TPU v7x, 1024 devices: a whole 4x8x16 slice. The times are simulated.
1024 devices in a mesh: fsdp: 32 (over y, x_lo, core), ep: 32 (over x_hi, z).
Axes of the slice: x: 4 (x_hi: 2, x_lo: 2; x = x_hi * 2 + x_lo), y: 8, z: 16, core: 2. Of those that a mesh axis runs over, the one named last changes fastest.
Arguments:
- expert_ids: int32 [1024, 4], P('ep'), may hold values from 0 to 15, all different within a row; in each aligned block of 32 rows (0 to 31, 32 to 63, ...) at most 16 rows name the same one
- route_weights: float32 [1024, 4], P('ep'), may hold values from 0.1 to 1
- residual_grad: bfloat16 [1024, 6144], P('ep', 'fsdp'), may hold values from -6 to 6
- hidden_grad: bfloat16 [32, 512, 2688], P('ep'), may hold values from -6 to 6
- gate_pre: bfloat16 [32, 512, 2688], P('ep'), may hold values from -6 to 6
- up_pre: bfloat16 [32, 512, 2688], P('ep'), may hold values from -6 to 6
- gate_weight: bfloat16 [32, 6144, 2688], P('ep', 'fsdp'), may hold values from -0.0625 to 0.0625
- up_weight: bfloat16 [32, 6144, 2688], P('ep', 'fsdp'), may hold values from -0.0625 to 0.0625
- attn_context: bfloat16 [8192, 6144], P('fsdp', 'ep'), may hold values from -6 to 6
- attn_grad: bfloat16 [8192, 6144], P('fsdp'), may hold values from -6 to 6
Outputs:
- input_grad: bfloat16 [1024, 6144], P('ep', 'fsdp')
- proj_weight_grad: float32 [6144, 6144], P('ep', 'fsdp')
Inputs may be any that keep to these rules, and one draw needn't show every extreme that they name: `expert_ids`: each row names 4 different experts. Among the rows of one ep index no expert is named more than 16 times, a bound that some block reaches.
All inputs are finite; a program needn't handle non-finite values.
Results may differ from a plain program's by a relative error of at most 0.005.
Values may be sent and summed in bfloat16 or wider, within the bound.
No kernel may reach another device: no remote copies, remote signals or barrier semaphores. Data moves between devices by JAX's collectives and lax.ppermute only.
A program may use at most 64 MiB of HBM per device.

v0:
```python
import jax
import jax.numpy as jnp
from jax import lax
from jax.sharding import PartitionSpec as P


def local_slots(expert_ids, experts):
    tokens, chosen = expert_ids.shape
    flat = expert_ids.reshape(tokens * chosen)
    onehot = (flat[:, None] == jnp.arange(experts, dtype=jnp.int32)[None, :]).astype(jnp.int32)
    before = jnp.cumsum(onehot, axis=0) - onehot
    return jnp.sum(before * onehot, axis=1).reshape(tokens, chosen)


def shards(
    expert_ids,
    route_weights,
    residual_grad,
    hidden_grad,
    gate_pre,
    up_pre,
    gate_weight,
    up_weight,
    attn_context,
    attn_grad,
):
    gate = gate_pre.astype(jnp.float32)
    upper = up_pre.astype(jnp.float32)
    grads = hidden_grad.astype(jnp.float32)
    sig = jax.nn.sigmoid(gate)
    up_term = (grads * gate * sig).astype(jnp.bfloat16)
    gate_term = (grads * upper * sig * (1.0 + gate * (1.0 - sig))).astype(jnp.bfloat16)
    rows_out = jnp.einsum(
        "brh,bdh->brd", gate_term, gate_weight, preferred_element_type=jnp.float32
    )
    rows_out = rows_out + jnp.einsum(
        "brh,bdh->brd", up_term, up_weight, preferred_element_type=jnp.float32
    )
    rows_out = rows_out.astype(jnp.bfloat16)
    received = lax.all_to_all(rows_out, "ep", split_axis=1, concat_axis=0, tiled=True)
    all_blocks, capacity, columns = received.shape
    received = received.reshape(all_blocks * capacity, columns).astype(jnp.float32)
    experts = all_blocks // 2
    slots = local_slots(expert_ids, experts)
    lower_col = 2 * expert_ids * capacity + slots
    upper_col = lower_col + capacity
    col_ids = jnp.arange(all_blocks * capacity, dtype=jnp.int32)[None, None, :]
    picks = (col_ids == lower_col[:, :, None]).astype(jnp.float32) + (
        col_ids == upper_col[:, :, None]
    ).astype(jnp.float32)
    combine = jnp.sum(route_weights[:, :, None] * picks, axis=1)
    gathered_sum = jnp.dot(combine, received, precision=lax.Precision.HIGHEST)
    input_grad = (residual_grad.astype(jnp.float32) + gathered_sum).astype(jnp.bfloat16)
    owned = lax.psum_scatter(
        jnp.einsum("tj,ti->ji", attn_grad, attn_context, preferred_element_type=jnp.float32),
        "fsdp",
        scatter_dimension=0,
        tiled=True,
    )
    proj_weight_grad = owned.T
    return (input_grad, proj_weight_grad)


def solution(mesh):
    return jax.shard_map(
        shards,
        mesh=mesh,
        in_specs=(
            P("ep", None),
            P("ep", None),
            P("ep", "fsdp"),
            P("ep", None, None),
            P("ep", None, None),
            P("ep", None, None),
            P("ep", "fsdp", None),
            P("ep", "fsdp", None),
            P("fsdp", "ep"),
            P("fsdp", None),
        ),
        out_specs=(P("ep", "fsdp"), P("ep", "fsdp")),
        check_vma=False,
    )
```

profile of v0, /device:TPU:4, one launch (start us, length us, event | category | flops | bytes accessed | tf_op | source)
XLA Modules:
  0.0 164.8 jit_solution(9513925690822900558)
XLA Ops:
  7.2 0.0 reduce-scatter.2.cloned.1.call-start
  7.2 1.8 %copy-done = bf16[256,6144]{1,0:T(8,128)(2,1)S(1)} copy-done((bf16[256,6144]{1,0:T(8,128)(2,1)S(1)}, bf16[256,6144]{1,0:T(8,128)(2,1)}, u32[]{:S(2)}) %copy-start) | copy-done | bytes 3145752
  9.1 4.6 %fusion.31 = f32[6144,192]{1,0:T(8,128)} fusion(bf16[256,6144]{1,0:T(8,128)(2,1)S(1)} %copy-done, bf16[256,192]{0,1:T(8,128)(2,1)} %param.18), kind=kOutput, calls=%fused_computation.35 | convolution fusion | flops 603979776 | bytes 7962624 | tf_op jit(solution)/shard_map/tj,ti->ji/dot_general | solution.py:55
  13.7 6.4 %fusion.11 = f32[512,192]{0,1:T(8,128)S(1)} fusion(bf16[1,512,2688]{2,1,0:T(8,128)(2,1)} %param.13, bf16[1,512,2688]{2,1,0:T(8,128)(2,1)} %param.14, bf16[1,512,2688]{2,1,0:T(8,128)(2,1)} %param.15, bf16[1,192,2688]{2,1,0:T(8,128)(2,1)} %param.16), kind=kOutput, calls=%fused_computation.15 | convolution fusion | flops 546373632 | bytes 9682944 | tf_op jit(solution)/shard_map/brh,bdh->brd/dot_general | solution.py:33
  20.2 1.9 %fusion.21 = bf16[1,512,192]{1,2,0:T(8,128)(2,1)S(1)} fusion(f32[512,192]{0,1:T(8,128)S(1)} %fusion.11, bf16[1,512,2688]{2,1,0:T(8,128)(2,1)S(1)} %copy-done.5, bf16[1,512,2688]{2,1,0:T(8,128)(2,1)S(1)} %copy-done.4, bf16[1,192,2688]{2,1,0:T(8,128)(2,1)S(1)} %copy-done.6), kind=kOutput, calls=%fused_computation.19 | convolution fusion | flops 539688960 | bytes 7127040 | tf_op jit(solution)/shard_map/brh,bdh->brd/dot_general | solution.py:36
  22.1 1.1 copy.45
  23.2 0.5 broadcast.32
  23.7 3.2 %reduce = bf16[512,192]{1,0:T(8,128)(2,1)S(1)} reduce(bf16[512,1,192]{2,1,0:T(2,128)(2,1)} %bitcast.29, bf16[]{:T(256)} %broadcast.32), dimensions={1}, to_apply=%bitcast.24.reduce_sub_computation | reduce | bytes 393218
  26.9 1.0 reshape.40
  27.9 21.9 %all-to-all-start = ((bf16[32,2,1536]{2,1,0:T(2,128)(2,1)}), bf16[32,2,1536]{2,1,0:T(2,128)(2,1)S(1)}, u32[]{:S(2)}, u32[]{:S(2)}) async-start(bf16[32,2,1536]{2,1,0:T(2,128)(2,1)} %reshape.40), calls=%async_computation | async-start | bytes 393216 | tf_op jit(solution)/shard_map/all_to_all | solution.py:40
  49.8 0.1 copy.43
  49.9 0.1 eq.42
  50.0 0.1 fusion.28
  50.1 0.2 reduce_window_sum.11
  50.2 0.2 select_reduce_fusion
  50.4 0.1 reshape.34
  50.5 0.1 copy.44
  50.6 0.1 multiply_reduce_fusion
  50.8 17.4 %all-to-all-done = bf16[32,2,1536]{2,1,0:T(2,128)(2,1)S(1)} async-done(((bf16[32,2,1536]{2,1,0:T(2,128)(2,1)}), bf16[32,2,1536]{2,1,0:T(2,128)(2,1)S(1)}, u32[]{:S(2)}, u32[]{:S(2)}) %all-to-all-start) | async-done | bytes 196640 | tf_op jit(solution)/shard_map/all_to_all | solution.py:40
  68.1 1.1 reshape.41
  69.2 1.2 copy.46
  70.4 0.9 fusion.24
  71.3 84.9 %reduce-scatter.2.cloned.1.call-done = f32[192,192]{1,0:T(8,128)} async-done(((f32[6144,192]{1,0:T(8,128)}), f32[192,192]{1,0:T(8,128)}) %reduce-scatter.2.cloned.1.call-update) | async-done | bytes 147472 | tf_op jit(solution)/shard_map/reduce_scatter | solution.py:54
  156.2 1.7 %copy.47 = f32[192,192]{1,0:T(8,128)} copy(f32[192,192]{0,1:T(8,128)} %bitcast.31) | data formatting | bytes 294912
  (15 shorter events, 0.1 us)
Async XLA Ops:
  7.2 1.9 %copy-start = (bf16[256,6144]{1,0:T(8,128)(2,1)S(1)}, bf16[256,6144]{1,0:T(8,128)(2,1)}, u32[]{:S(2)}) copy-start(bf16[256,6144]{1,0:T(8,128)(2,1)} %param.19) | copy-start | bytes 9437188
  7.2 149.0 %reduce-scatter.2.cloned.1.call-start = ((), (), s32[]{:S(2)}) async-start(), calls=%async_computation.2 | async-start | bytes 6488064 | tf_op jit(solution)/shard_map/reduce_scatter | solution.py:54
  13.7 6.4 %copy-start.4 = (bf16[1,512,2688]{2,1,0:T(8,128)(2,1)S(1)}, bf16[1,512,2688]{2,1,0:T(8,128)(2,1)}, u32[]{:S(2)}) copy-start(bf16[1,512,2688]{2,1,0:T(8,128)(2,1)} %param.13) | copy-start | bytes 8257540
  13.7 6.4 %copy-start.5 = (bf16[1,512,2688]{2,1,0:T(8,128)(2,1)S(1)}, bf16[1,512,2688]{2,1,0:T(8,128)(2,1)}, u32[]{:S(2)}) copy-start(bf16[1,512,2688]{2,1,0:T(8,128)(2,1)} %param.14) | copy-start | bytes 8257540
  13.7 6.4 %copy-start.6 = (bf16[1,192,2688]{2,1,0:T(8,128)(2,1)S(1)}, bf16[1,192,2688]{2,1,0:T(8,128)(2,1)}, u32[]{:S(2)}) copy-start(bf16[1,192,2688]{2,1,0:T(8,128)(2,1)} %param.17) | copy-start | bytes 3096580
  20.1 29.6 %copy-start.2 = (s32[32,4]{0,1:T(4,128)S(1)}, s32[32,4]{0,1:T(4,128)}, u32[]{:S(2)}) copy-start(s32[32,4]{0,1:T(4,128)} %param.10) | copy-start | bytes 1540
  20.2 30.5 %copy-start.3 = (f32[32,4]{0,1:T(4,128)S(1)}, f32[32,4]{0,1:T(4,128)}, u32[]{:S(2)}) copy-start(f32[32,4]{0,1:T(4,128)} %param.11) | copy-start | bytes 1540
  20.2 50.3 %copy-start.1 = (bf16[32,192]{1,0:T(8,128)(2,1)S(1)}, bf16[32,192]{1,0:T(8,128)(2,1)}, u32[]{:S(2)}) copy-start(bf16[32,192]{1,0:T(8,128)(2,1)} %param.12) | copy-start | bytes 36868
  27.9 40.3 %all-to-all-start = ((bf16[32,2,1536]{2,1,0:T(2,128)(2,1)}), bf16[32,2,1536]{2,1,0:T(2,128)(2,1)S(1)}, u32[]{:S(2)}, u32[]{:S(2)}) async-start(bf16[32,2,1536]{2,1,0:T(2,128)(2,1)} %reshape.40), calls=%async_computation | async-start | bytes 393216 | tf_op jit(solution)/shard_map/all_to_all | solution.py:40
Sparse Core Ops, SparseCore 0:
  13.8 142.3 reduce-scatter.1
where the time goes:
time: 165 us
  waiting for transfers between devices  102 us (62%)
  starting transfers between devices  21.9 us (13%)
  between operations  14.2 us (9%)
  matrix products  13.8 us (8%)
  local copies, waits for them, and re-layouts  8.85 us (5%)
  other arithmetic  3.77 us (2%)
    reduce_scatter x1, waiting for transfers between devices, shards(): lax.psum_scatter(jnp.einsum('tj,ti->ji', attn_grad, attn_context, preferr...  84.9 us
    all_to_all x1, starting transfers between devices, shards(): lax.all_to_all(rows_out, 'ep', split_axis=1, concat_axis=0, tiled=True)  21.9 us
    all_to_all x1, waiting for transfers between devices, shards(): lax.all_to_all(rows_out, 'ep', split_axis=1, concat_axis=0, tiled=True)  17.4 us
    dot_general x1, matrix products, shards(): jnp.einsum('brh,bdh->brd', gate_term, gate_weight, preferred_element_type...  6.39 us
    unnamed x19, local copies, waits for them, and re-layouts  6.26 us
    dot_general x1, matrix products, shards(): jnp.einsum('tj,ti->ji', attn_grad, attn_context, preferred_element_type=j...  4.59 us
  transfers between devices with their start and end apart: 2, of which 2 were waited for; matrix products, arithmetic and copies ran while one was open for 11% of the time, Pallas kernels for 0%

commit v1 on v0

v1 whole, which is shorter than its diff:
```python
import functools

import jax
import jax.numpy as jnp
from jax import lax
from jax.experimental import pallas as pl
from jax.experimental.pallas import tpu as pltpu
from jax.sharding import PartitionSpec as P

F32, BF16 = jnp.float32, jnp.bfloat16
LANES = 128
MIB = 1 << 20


def params(limit=32 * MIB):
    return pltpu.CompilerParams(vmem_limit_bytes=limit)


def whole():
    return pl.BlockSpec(memory_space=pltpu.VMEM)


def low_lanes(rows):
    return lax.broadcasted_iota(jnp.int32, (rows, LANES), 1) < LANES // 2


def proj_partial_kernel(core_ref, ctx_ref, grad_ref, own_ref, send_ref):
    rows = ctx_ref.shape[1]
    half = rows // 2
    full = rows + half
    core = core_ref[0]
    left = low_lanes(half)
    for pair in range(grad_ref.shape[1] // (2 * rows)):
        cols = grad_ref[:, pair * 2 * rows:(pair + 1) * 2 * rows]
        prod = lax.dot_general(
            ctx_ref[...], cols, (((0,), (0,)), ((), ())), preferred_element_type=F32
        )
        middle = prod[:, LANES:2 * LANES]
        upper, lower = middle[:half], middle[half:]
        even = jnp.concatenate(
            [prod[:, :LANES], jnp.where(left, upper, pltpu.roll(lower, LANES // 2, 1))], axis=0
        )
        odd = jnp.concatenate(
            [prod[:, 2 * LANES:], jnp.where(left, pltpu.roll(upper, LANES // 2, 1), lower)], axis=0
        )
        at = slice(pair * full, (pair + 1) * full)
        own_ref[at, :] = jnp.where(core == 0, even, odd).astype(own_ref.dtype)
        send_ref[at, :] = jnp.where(core == 0, odd, even).astype(send_ref.dtype)


def proj_partial(core, ctx, grad):
    tokens, rows = ctx.shape
    steps = 4
    width = grad.shape[1] // steps
    out_rows = grad.shape[1] * rows // LANES
    return pl.pallas_call(
        proj_partial_kernel,
        grid=(steps,),
        in_specs=[
            pl.BlockSpec(memory_space=pltpu.SMEM),
            pl.BlockSpec((tokens, rows), lambda s: (0, 0)),
            pl.BlockSpec((tokens, width), lambda s: (0, s)),
        ],
        out_specs=[pl.BlockSpec((out_rows // 2 // steps, LANES), lambda s: (s, 0))] * 2,
        out_shape=[jax.ShapeDtypeStruct((out_rows // 2, LANES), BF16)] * 2,
        compiler_params=params(),
        cost_estimate=pl.CostEstimate(
            flops=2 * tokens * rows * grad.shape[1], bytes_accessed=6 * MIB, transcendentals=0
        ),
        name="proj_partial",
    )(core, ctx, grad)


def chip_sum_kernel(side_ref, own_ref, got_ref, keep_ref, send_ref, by_y_ref, *, rows):
    side = side_ref[0]
    half = rows // 2
    full = rows + half
    for y in range(keep_ref.shape[0] // rows):
        mine = pl.ds(pl.multiple_of((2 * y + side) * full, 16), rows)
        other = pl.ds(pl.multiple_of((2 * y + 1 - side) * full, 16), rows)
        at = slice(y * rows, (y + 1) * rows)
        keep_ref[at, :] = own_ref[mine, :] + got_ref[mine, :].astype(F32)
        send_ref[at, :] = (own_ref[other, :] + got_ref[other, :].astype(F32)).astype(BF16)
        for x in range(2):
            start = (2 * y + x) * full + rows
            block = slice(start, start + half)
            to = slice((2 * y + x) * half, (2 * y + x + 1) * half)
            by_y_ref[to, :] = (own_ref[block, :] + got_ref[block, :].astype(F32)).astype(BF16)


def add_kernel(own_ref, got_ref, out_ref):
    out_ref[...] = (own_ref[...] + got_ref[...].astype(F32)).astype(out_ref.dtype)


def y_sum_kernel(side_ref, got_ref, keep_ref, send_ref, *, parts):
    rows = got_ref.shape[0] // parts
    half = rows // 2
    side = side_ref[0]

    def total(start):
        acc = got_ref[pl.ds(start, half), :].astype(F32)
        for part in range(1, parts):
            acc += got_ref[pl.ds(part * rows + start, half), :].astype(F32)
        return acc

    keep_ref[...] = total(pl.multiple_of(side * half, 16))
    send_ref[...] = total(pl.multiple_of((1 - side) * half, 16)).astype(BF16)


def proj_final_kernel(core_ref, main_ref, keep_ref, got_ref, out_ref, *, parts):
    rows = main_ref.shape[0] // parts
    core = core_ref[0]
    acc = main_ref[:rows, :].astype(F32)
    for part in range(1, parts):
        acc += main_ref[part * rows:(part + 1) * rows, :].astype(F32)
    packed = keep_ref[...] + got_ref[...].astype(F32)
    half = jnp.concatenate([packed, pltpu.roll(packed, LANES // 2, 1)], axis=0)
    turned = pltpu.roll(acc, LANES // 2, 1)
    out_ref[:, :LANES] = jnp.where(core == 0, acc, jnp.where(low_lanes(rows), half, turned))
    out_ref[:, LANES:] = jnp.where(core == 0, half, turned)[:, :rows - LANES]


def expert_kernel(hid_ref, gate_ref, up_ref, gw_ref, uw_ref, out_ref, acc_ref):
    step = pl.program_id(0)
    hid = hid_ref[...].astype(F32)
    gate = gate_ref[...].astype(F32)
    sig = 0.5 * jnp.tanh(0.5 * gate) + 0.5
    scaled = hid * sig
    up_term = (scaled * gate).astype(BF16)
    gate_term = (scaled * up_ref[...].astype(F32) * (1.0 + gate * (1.0 - sig))).astype(BF16)
    dims = (((1,), (1,)), ((), ()))
    prod = lax.dot_general(gate_term, gw_ref[...], dims, preferred_element_type=F32)
    prod += lax.dot_general(up_term, uw_ref[...], dims, preferred_element_type=F32)

    @pl.when(step == 0)
    def _():
        acc_ref[...] = prod

    @pl.when(step > 0)
    def _():
        acc_ref[...] += prod

    @pl.when(step == pl.num_programs(0) - 1)
    def _():
        slots, width = acc_ref.shape
        rest = width - LANES
        groups = slots // 16
        main = acc_ref[:, :LANES].reshape(groups, 16, LANES)
        side = acc_ref[:, LANES:].reshape(groups, 2, 8, rest)
        side = jnp.concatenate([side[:, 0], side[:, 1]], axis=-1)
        packed = jnp.concatenate([main, side], axis=1)
        out_ref[...] = packed.reshape(groups * 24, LANES).astype(BF16)


def expert_rows(hid, gate, up, gw, uw):
    slots, hidden = hid.shape
    width = gw.shape[0]
    block = 384
    steps = hidden // block
    rows_spec = pl.BlockSpec((slots, block), lambda s: (0, s))
    weight_spec = pl.BlockSpec((width, block), lambda s: (0, s))
    out_rows = slots * width // LANES
    return pl.pallas_call(
        expert_kernel,
        grid=(steps,),
        in_specs=[rows_spec] * 3 + [weight_spec] * 2,
        out_specs=pl.BlockSpec((out_rows, LANES), lambda s: (0, 0)),
        out_shape=jax.ShapeDtypeStruct((out_rows, LANES), BF16),
        scratch_shapes=[pltpu.VMEM((slots, width), F32)],
        compiler_params=params(),
        cost_estimate=pl.CostEstimate(
            flops=4 * slots * hidden * width,
            bytes_accessed=2 * hidden * (3 * slots + 2 * width),
            transcendentals=slots * hidden,
        ),
        name="expert_rows",
    )(hid, gate, up, gw, uw)


def combine_kernel(ids_ref, weights_ref, residual_ref, got_ref, out_ref):
    tokens, top = ids_ref.shape
    blocks = got_ref.shape[0] // 24
    experts = blocks // 2
    ids, weights = ids_ref[...], weights_ref[...]
    row = lax.broadcasted_iota(jnp.int32, (tokens, tokens), 0)
    col = lax.broadcasted_iota(jnp.int32, (tokens, tokens), 1)
    earlier = (col < row).astype(F32)

    def picks(per_expert):
        lane = lax.broadcasted_iota(jnp.int32, (tokens, experts * per_expert), 1)
        named = jnp.zeros(lane.shape, F32)
        weight = jnp.zeros(lane.shape, F32)
        for k in range(top):
            hit = ids[:, k:k + 1] == lane // per_expert
            named += hit.astype(F32)
            weight += jnp.where(hit, weights[:, k:k + 1], 0.0)
        before = jnp.dot(earlier, named, preferred_element_type=F32)
        slot = (lane % per_expert).astype(F32)
        return [
            jnp.where(before == slot + base, weight, 0.0) for base in range(0, 16, per_expert)
        ]

    got = got_ref[...].astype(F32).reshape(experts, 2, 24, LANES)
    both = got[:, 0] + got[:, 1]
    main = both[:, :16].reshape(experts * 16, LANES)
    side = both[:, 16:].reshape(experts * 8, LANES)
    dot = functools.partial(
        jnp.dot, precision=lax.Precision.HIGHEST, preferred_element_type=F32
    )
    first, second = picks(8)
    main_sum = dot(picks(16)[0], main)
    side_sum = dot(first, side) + pltpu.roll(dot(second, side), LANES // 2, 1)
    rest = out_ref.shape[1] - LANES
    out_ref[:, :LANES] = (residual_ref[:, :LANES].astype(F32) + main_sum).astype(BF16)
    out_ref[:, LANES:] = (residual_ref[:, LANES:].astype(F32) + side_sum[:, :rest]).astype(BF16)


def shards(ids, weights, residual, hid, gate, up, gw, uw, ctx, grad, n_fsdp):
    me = lax.axis_index("fsdp")
    core = (me & 1).reshape(1)
    side = ((me >> 1) & 1).reshape(1)
    rows = ctx.shape[1]
    half = rows // 2
    n_y = n_fsdp // 4
    y_groups = [[4 * y + c for y in range(n_y)] for c in range(4)]
    along_core = [(j, j ^ 1) for j in range(n_fsdp)]
    along_x = [(j, j ^ 2) for j in range(n_fsdp)]

    def swap(array, pairs):
        return lax.ppermute(array, "fsdp", pairs)

    def to_y(array):
        return lax.all_to_all(
            array, "fsdp", 0, 0, axis_index_groups=y_groups, tiled=True
        )

    own, send = proj_partial(core, ctx, grad)
    got = swap(send, along_core)
    rows_out = expert_rows(hid[0], gate[0], up[0], gw[0], uw[0])
    received = lax.all_to_all(rows_out, "ep", 0, 0, tiled=True)

    smem = pl.BlockSpec(memory_space=pltpu.SMEM)
    wide = jax.ShapeDtypeStruct((n_y * rows, LANES), BF16)
    keep, x_send, by_y = pl.pallas_call(
        functools.partial(chip_sum_kernel, rows=rows),
        in_specs=[smem, whole(), whole()],
        out_specs=[whole()] * 3,
        out_shape=[jax.ShapeDtypeStruct(wide.shape, F32), wide, wide],
        compiler_params=params(),
        name="chip_sum",
    )(side, own, got)
    x_got = swap(x_send, along_x)
    side_parts = to_y(by_y)
    main_send = pl.pallas_call(
        add_kernel,
        in_specs=[whole()] * 2,
        out_specs=whole(),
        out_shape=wide,
        compiler_params=params(),
        name="x_sum",
    )(keep, x_got)
    main_parts = to_y(main_send)
    side_keep, side_send = pl.pallas_call(
        functools.partial(y_sum_kernel, parts=n_y),
        in_specs=[smem, whole()],
        out_specs=[whole()] * 2,
        out_shape=[
            jax.ShapeDtypeStruct((half, LANES), F32),
            jax.ShapeDtypeStruct((half, LANES), BF16),
        ],
        compiler_params=params(),
        name="y_sum",
    )(side, side_parts)
    side_got = swap(side_send, along_x)

    input_grad = pl.pallas_call(
        combine_kernel,
        in_specs=[whole()] * 4,
        out_specs=whole(),
        out_shape=jax.ShapeDtypeStruct(residual.shape, BF16),
        compiler_params=params(),
        name="combine",
    )(ids, weights, residual, received)
    proj_weight_grad = pl.pallas_call(
        functools.partial(proj_final_kernel, parts=n_y),
        in_specs=[smem] + [whole()] * 3,
        out_specs=whole(),
        out_shape=jax.ShapeDtypeStruct((rows, rows), F32),
        compiler_params=params(),
        name="proj_final",
    )(core, main_parts, side_keep, side_got)
    return input_grad, proj_weight_grad


def solution(mesh):
    return jax.shard_map(
        functools.partial(shards, n_fsdp=mesh.shape["fsdp"]),
        mesh=mesh,
        in_specs=(
            P("ep", None),
            P("ep", None),
            P("ep", "fsdp"),
            P("ep", None, None),
            P("ep", None, None),
            P("ep", None, None),
            P("ep", "fsdp", None),
            P("ep", "fsdp", None),
            P("fsdp", "ep"),
            P("fsdp", None),
        ),
        out_specs=(P("ep", "fsdp"), P("ep", "fsdp")),
        check_vma=False,
    )
```

time: 165 us -> 103 us (0.62)
  the two profiles are of different devices: /device:TPU:4 before, /device:TPU:64 now
where the time goes in v1:
time: 103 us; the launch traced here: 102 us
  starting transfers between devices  40.8 us (40%)
  waiting for transfers between devices  38 us (37%)
  Pallas kernels  12.3 us (12%)
  local copies, waits for them, and re-layouts  10.6 us (10%)
    all_to_all x1, starting transfers between devices, shards(): received = lax.all_to_all(rows_out, 'ep', 0, 0, tiled=True)  21 us
    all_to_all x1, waiting for transfers between devices, shards(): received = lax.all_to_all(rows_out, 'ep', 0, 0, tiled=True)  18.6 us
    all_to_all x2, starting transfers between devices, to_y(): lax.all_to_all(array, 'fsdp', 0, 0, axis_index_groups=y_groups, tiled=True)  12.8 us
    ppermute x3, waiting for transfers between devices, swap(): return lax.ppermute(array, 'fsdp', pairs)  11.4 us
    unnamed x25, local copies, waits for them, and re-layouts  10.6 us
    all_to_all x2, waiting for transfers between devices, to_y(): lax.all_to_all(array, 'fsdp', 0, 0, axis_index_groups=y_groups, tiled=True)  7.96 us
    ppermute x3, starting transfers between devices, swap(): return lax.ppermute(array, 'fsdp', pairs)  6.9 us
    pallas_call x1, Pallas kernels, expert_rows(): pl.pallas_call(expert_kernel, grid=(steps,), in_specs=[rows_spec] * 3 + [...  6.19 us
  transfers between devices with their start and end apart: 6, of which 5 were waited for; matrix products, arithmetic and copies ran while one was open for 0% of the time, Pallas kernels for 8%

profile of v1, /device:TPU:64, one launch (start us, length us, event | category | flops | bytes accessed | tf_op | source)
XLA Modules:
  0.0 102.4 jit_solution(5184481828791170790)
XLA Ops:
  0.6 1.0 copy.14.ctx_ref
  1.6 1.9 %copy-done = bf16[256,6144]{1,0:T(8,128)(2,1)S(1)} copy-done((bf16[256,6144]{1,0:T(8,128)(2,1)S(1)}, bf16[256,6144]{1,0:T(8,128)(2,1)}, u32[]{:S(2)}) %copy-start) | copy-done | bytes 3145752
  3.5 3.1 %proj_partial.1 = (bf16[4608,128]{1,0:T(8,128)(2,1)S(1)}, bf16[4608,128]{1,0:T(8,128)(2,1)}) custom-call(s32[1]{0:T(128)} %bitcast.7.core_ref, bf16[256,192]{1,0:T(8,128)(2,1)S(1)} %copy.14.ctx_ref, bf16[256,6144]{1,0:T(8,128)(2,1)S(1)} %copy-done), custom_call_target="tpu_custom_call" | custom-call | flops 603979776 | bytes 6291456 | tf_op jit(solution)/shard_map/proj_partial/pallas_call | solution.py:56
  6.6 1.9 %collective-permute-start = (bf16[4608,128]{1,0:T(8,128)(2,1)}, bf16[4608,128]{1,0:T(8,128)(2,1)S(1)}, u32[]{:S(2)}, u32[]{:S(2)}) collective-permute-start(bf16[4608,128]{1,0:T(8,128)(2,1)} %get-tuple-element.10), channel_id=1, source_target_pairs={{0,32},{32,0},{64,96},{96,64},{128,160},{160,128},{192,224},{224,1... | collective-permute-start | bytes 3538952 | tf_op jit(solution)/shard_map/ppermute | solution.py:230
  8.5 1.8 %copy-done.2 = bf16[1,512,2688]{2,1,0:T(8,128)(2,1)S(1)} copy-done((bf16[1,512,2688]{2,1,0:T(8,128)(2,1)S(1)}, bf16[1,512,2688]{2,1,0:T(8,128)(2,1)}, u32[]{:S(2)}) %copy-start.2) | copy-done | bytes 2752536
  10.3 1.8 %copy-done.3 = bf16[1,512,2688]{2,1,0:T(8,128)(2,1)S(1)} copy-done((bf16[1,512,2688]{2,1,0:T(8,128)(2,1)S(1)}, bf16[1,512,2688]{2,1,0:T(8,128)(2,1)}, u32[]{:S(2)}) %copy-start.3) | copy-done | bytes 2752536
  12.1 1.2 %copy-done.4 = bf16[1,192,2688]{2,1,0:T(8,128)(2,1)S(1)} copy-done((bf16[1,192,2688]{2,1,0:T(8,128)(2,1)S(1)}, bf16[1,192,2688]{2,1,0:T(8,128)(2,1)}, u32[]{:S(2)}) %copy-start.4) | copy-done | bytes 1032216
  13.3 1.2 %copy-done.5 = bf16[1,192,2688]{2,1,0:T(8,128)(2,1)S(1)} copy-done((bf16[1,192,2688]{2,1,0:T(8,128)(2,1)S(1)}, bf16[1,192,2688]{2,1,0:T(8,128)(2,1)}, u32[]{:S(2)}) %copy-start.5) | copy-done | bytes 1032216
  14.5 6.2 %expert_rows.1 = bf16[768,128]{1,0:T(8,128)(2,1)} custom-call(bf16[512,2688]{1,0:T(8,128)(2,1)S(1)} %bitcast.13, bf16[512,2688]{1,0:T(8,128)(2,1)S(1)} %bitcast.14, bf16[512,2688]{1,0:T(8,128)(2,1)S(1)} %bitcast.15, bf16[192,2688]{1,0:T(8,128)(2,1)S(1)} %bitcast.18, bf16[192,2688]{1,0:T(8,128)(2,1)S(1)} %bitcast.19), custom_call_target="tpu_custom_call" | custom-call | flops 1056964608 | bytes 10321920 | tf_op jit(solution)/shard_map/expert_rows/pallas_call | solution.py:163
  20.7 21.0 %all-to-all-start = ((bf16[32,24,128]{2,1,0:T(8,128)(2,1)}), bf16[32,24,128]{2,1,0:T(8,128)(2,1)S(1)}, u32[]{:S(2)}, u32[]{:S(2)}) async-start(bf16[32,24,128]{2,1,0:T(8,128)(2,1)} %bitcast.5), calls=%async_computation | async-start | bytes 393216 | tf_op jit(solution)/shard_map/all_to_all | solution.py:240
  42.1 0.7 copy-done.6
  42.8 0.7 copy-done.8
  43.6 18.6 %all-to-all-done = bf16[32,24,128]{2,1,0:T(8,128)(2,1)S(1)} async-done(((bf16[32,24,128]{2,1,0:T(8,128)(2,1)}), bf16[32,24,128]{2,1,0:T(8,128)(2,1)S(1)}, u32[]{:S(2)}, u32[]{:S(2)}) %all-to-all-start) | async-done | bytes 196640 | tf_op jit(solution)/shard_map/all_to_all | solution.py:240
  62.2 7.1 %all-to-all-start.2 = ((bf16[8,192,128]{2,1,0:T(8,128)(2,1)}), bf16[8,192,128]{2,1,0:T(8,128)(2,1)S(1)}, u32[]{:S(2)}, u32[]{:S(2)}) async-start(bf16[8,192,128]{2,1,0:T(8,128)(2,1)} %bitcast.21), calls=%async_computation.2 | async-start | bytes 786432 | tf_op jit(solution)/shard_map/all_to_all | solution.py:233
  69.3 2.5 %collective-permute-start.1 = (bf16[1536,128]{1,0:T(8,128)(2,1)}, bf16[1536,128]{1,0:T(8,128)(2,1)S(1)}, u32[]{:S(2)}, u32[]{:S(2)}) collective-permute-start(bf16[1536,128]{1,0:T(8,128)(2,1)} %copy-done.8), channel_id=1, source_target_pairs={{0,64},{32,96},{64,0},{96,32},{128,192},{160,224},{192,128},{224,1... | collective-permute-start | bytes 1179656 | tf_op jit(solution)/shard_map/ppermute | solution.py:230
  71.8 9.5 %collective-permute-done.1.got_ref = bf16[1536,128]{1,0:T(8,128)(2,1)S(1)} collective-permute-done((bf16[1536,128]{1,0:T(8,128)(2,1)}, bf16[1536,128]{1,0:T(8,128)(2,1)S(1)}, u32[]{:S(2)}, u32[]{:S(2)}) %collective-permute-start.1) | collective-permute-done | bytes 393248 | tf_op jit(solution)/shard_map/ppermute | solution.py:230
  81.3 0.8 x_sum.1
  82.1 1.2 %all-to-all-done.2 = bf16[8,192,128]{2,1,0:T(8,128)(2,1)S(1)} async-done(((bf16[8,192,128]{2,1,0:T(8,128)(2,1)}), bf16[8,192,128]{2,1,0:T(8,128)(2,1)S(1)}, u32[]{:S(2)}, u32[]{:S(2)}) %all-to-all-start.2) | async-done | bytes 393248 | tf_op jit(solution)/shard_map/all_to_all | solution.py:233
  83.3 5.7 %all-to-all-start.1 = ((bf16[8,192,128]{2,1,0:T(8,128)(2,1)}), bf16[8,192,128]{2,1,0:T(8,128)(2,1)S(1)}, u32[]{:S(2)}, u32[]{:S(2)}) async-start(bf16[8,192,128]{2,1,0:T(8,128)(2,1)} %bitcast.9), calls=%async_computation.1 | async-start | bytes 786432 | tf_op jit(solution)/shard_map/all_to_all | solution.py:233
  89.1 2.5 %collective-permute-start.2 = (bf16[96,128]{1,0:T(8,128)(2,1)S(1)}, bf16[96,128]{1,0:T(8,128)(2,1)S(1)}, u32[]{:S(2)}, u32[]{:S(2)}) collective-permute-start(bf16[96,128]{1,0:T(8,128)(2,1)S(1)} %get-tuple-element.15), channel_id=1, source_target_pairs={{0,64},{32,96},{64,0},{96,32},{128,192},{160,224},{192,128},{224,1... | collective-permute-start | bytes 73736 | tf_op jit(solution)/shard_map/ppermute | solution.py:230
  91.8 1.2 %combine.1 = bf16[32,192]{1,0:T(8,128)(2,1)} custom-call(s32[32,4]{1,0:T(8,128)S(1)} %copy.12.ids_ref, f32[32,4]{1,0:T(8,128)S(1)} %copy.13.weights_ref, bf16[32,192]{1,0:T(8,128)(2,1)S(1)} %copy-done.7, bf16[768,128]{1,0:T(8,128)(2,1)S(1)} %bitcast.20), custom_call_target="tpu_custom_call" | custom-call | tf_op jit(solution)/shard_map/combine/pallas_call | solution.py:276
  93.0 1.9 %collective-permute-done.2.got_ref = bf16[96,128]{1,0:T(8,128)(2,1)S(1)} collective-permute-done((bf16[96,128]{1,0:T(8,128)(2,1)S(1)}, bf16[96,128]{1,0:T(8,128)(2,1)S(1)}, u32[]{:S(2)}, u32[]{:S(2)}) %collective-permute-start.2) | collective-permute-done | bytes 24608 | tf_op jit(solution)/shard_map/ppermute | solution.py:230
  94.8 6.8 %all-to-all-done.1 = bf16[8,192,128]{2,1,0:T(8,128)(2,1)S(1)} async-done(((bf16[8,192,128]{2,1,0:T(8,128)(2,1)}), bf16[8,192,128]{2,1,0:T(8,128)(2,1)S(1)}, u32[]{:S(2)}, u32[]{:S(2)}) %all-to-all-start.1) | async-done | bytes 393248 | tf_op jit(solution)/shard_map/all_to_all | solution.py:233
  101.6 0.8 proj_final.1
  (20 shorter events, 0.5 us)
Async XLA Ops:
  1.6 1.9 %copy-start = (bf16[256,6144]{1,0:T(8,128)(2,1)S(1)}, bf16[256,6144]{1,0:T(8,128)(2,1)}, u32[]{:S(2)}) copy-start(bf16[256,6144]{1,0:T(8,128)(2,1)} %grad_ref.1) | copy-start | bytes 9437188
  3.5 5.0 %copy-start.1 = (bf16[1,512,2688]{2,1,0:T(8,128)(2,1)S(1)}, bf16[1,512,2688]{2,1,0:T(8,128)(2,1)}, u32[]{:S(2)}) copy-start(bf16[1,512,2688]{2,1,0:T(8,128)(2,1)} %param.13) | copy-start | bytes 8257540
  6.6 35.2 %collective-permute-start = (bf16[4608,128]{1,0:T(8,128)(2,1)}, bf16[4608,128]{1,0:T(8,128)(2,1)S(1)}, u32[]{:S(2)}, u32[]{:S(2)}) collective-permute-start(bf16[4608,128]{1,0:T(8,128)(2,1)} %get-tuple-element.10), channel_id=1, source_target_pairs={{0,32},{32,0},{64,96},{96,64},{128,160},{160,128},{192,224},{224,1... | collective-permute-start | bytes 3538952 | tf_op jit(solution)/shard_map/ppermute | solution.py:230
  8.5 1.8 %copy-start.2 = (bf16[1,512,2688]{2,1,0:T(8,128)(2,1)S(1)}, bf16[1,512,2688]{2,1,0:T(8,128)(2,1)}, u32[]{:S(2)}) copy-start(bf16[1,512,2688]{2,1,0:T(8,128)(2,1)} %param.14) | copy-start | bytes 8257540
  10.3 1.8 %copy-start.3 = (bf16[1,512,2688]{2,1,0:T(8,128)(2,1)S(1)}, bf16[1,512,2688]{2,1,0:T(8,128)(2,1)}, u32[]{:S(2)}) copy-start(bf16[1,512,2688]{2,1,0:T(8,128)(2,1)} %param.15) | copy-start | bytes 8257540
  12.1 1.2 %copy-start.4 = (bf16[1,192,2688]{2,1,0:T(8,128)(2,1)S(1)}, bf16[1,192,2688]{2,1,0:T(8,128)(2,1)}, u32[]{:S(2)}) copy-start(bf16[1,192,2688]{2,1,0:T(8,128)(2,1)} %param.16) | copy-start | bytes 3096580
  13.3 1.2 %copy-start.5 = (bf16[1,192,2688]{2,1,0:T(8,128)(2,1)S(1)}, bf16[1,192,2688]{2,1,0:T(8,128)(2,1)}, u32[]{:S(2)}) copy-start(bf16[1,192,2688]{2,1,0:T(8,128)(2,1)} %param.17) | copy-start | bytes 3096580
  20.7 41.5 %all-to-all-start = ((bf16[32,24,128]{2,1,0:T(8,128)(2,1)}), bf16[32,24,128]{2,1,0:T(8,128)(2,1)S(1)}, u32[]{:S(2)}, u32[]{:S(2)}) async-start(bf16[32,24,128]{2,1,0:T(8,128)(2,1)} %bitcast.5), calls=%async_computation | async-start | bytes 393216 | tf_op jit(solution)/shard_map/all_to_all | solution.py:240
  41.8 49.9 %copy-start.9 = (s32[32,4]{0,1:T(4,128)S(1)}, s32[32,4]{0,1:T(4,128)}, u32[]{:S(2)}) copy-start(s32[32,4]{0,1:T(4,128)} %param.10) | copy-start | bytes 1540
  41.8 49.9 %copy-start.10 = (f32[32,4]{0,1:T(4,128)S(1)}, f32[32,4]{0,1:T(4,128)}, u32[]{:S(2)}) copy-start(f32[32,4]{0,1:T(4,128)} %param.11) | copy-start | bytes 1540
  41.8 50.0 %copy-start.7 = (bf16[32,192]{1,0:T(8,128)(2,1)S(1)}, bf16[32,192]{1,0:T(8,128)(2,1)}, u32[]{:S(2)}) copy-start(bf16[32,192]{1,0:T(8,128)(2,1)} %residual_ref.1) | copy-start | bytes 36868
  42.1 0.8 copy-start.6
  42.8 0.7 copy-start.8
  62.2 21.1 %all-to-all-start.2 = ((bf16[8,192,128]{2,1,0:T(8,128)(2,1)}), bf16[8,192,128]{2,1,0:T(8,128)(2,1)S(1)}, u32[]{:S(2)}, u32[]{:S(2)}) async-start(bf16[8,192,128]{2,1,0:T(8,128)(2,1)} %bitcast.21), calls=%async_computation.2 | async-start | bytes 786432 | tf_op jit(solution)/shard_map/all_to_all | solution.py:233
  69.3 12.0 %collective-permute-start.1 = (bf16[1536,128]{1,0:T(8,128)(2,1)}, bf16[1536,128]{1,0:T(8,128)(2,1)S(1)}, u32[]{:S(2)}, u32[]{:S(2)}) collective-permute-start(bf16[1536,128]{1,0:T(8,128)(2,1)} %copy-done.8), channel_id=1, source_target_pairs={{0,64},{32,96},{64,0},{96,32},{128,192},{160,224},{192,128},{224,1... | collective-permute-start | bytes 1179656 | tf_op jit(solution)/shard_map/ppermute | solution.py:230
  83.3 18.3 %all-to-all-start.1 = ((bf16[8,192,128]{2,1,0:T(8,128)(2,1)}), bf16[8,192,128]{2,1,0:T(8,128)(2,1)S(1)}, u32[]{:S(2)}, u32[]{:S(2)}) async-start(bf16[8,192,128]{2,1,0:T(8,128)(2,1)} %bitcast.9), calls=%async_computation.1 | async-start | bytes 786432 | tf_op jit(solution)/shard_map/all_to_all | solution.py:233
  89.1 5.7 %collective-permute-start.2 = (bf16[96,128]{1,0:T(8,128)(2,1)S(1)}, bf16[96,128]{1,0:T(8,128)(2,1)S(1)}, u32[]{:S(2)}, u32[]{:S(2)}) collective-permute-start(bf16[96,128]{1,0:T(8,128)(2,1)S(1)} %get-tuple-element.15), channel_id=1, source_target_pairs={{0,64},{32,96},{64,0},{96,32},{128,192},{160,224},{192,128},{224,1... | collective-permute-start | bytes 73736 | tf_op jit(solution)/shard_map/ppermute | solution.py:230

commit v2 on v0

v2 whole, which is shorter than its diff:
```python
import functools

import jax
import jax.numpy as jnp
from jax import lax
from jax.experimental import pallas as pl
from jax.experimental.pallas import tpu as pltpu
from jax.sharding import PartitionSpec as P

F32, BF16 = jnp.float32, jnp.bfloat16
LANES = 128
MIB = 1 << 20
EXPERTS = 16
GRAD_PARTS = 2
HIDDEN_PART = 768


def params(limit):
    return pltpu.CompilerParams(vmem_limit_bytes=limit)


def whole():
    return pl.BlockSpec(memory_space=pltpu.VMEM)


def in_hbm():
    return pl.BlockSpec(memory_space=pltpu.HBM)


def hold(array):
    return pltpu.with_memory_space_constraint(array, pltpu.HBM)


def low_lanes(rows):
    return lax.broadcasted_iota(jnp.int32, (rows, LANES), 1) < LANES // 2


def write_picks(ids, weights, picks_ref):
    top, tokens = ids.shape
    row = lax.broadcasted_iota(jnp.int32, (tokens, tokens), 0)
    col = lax.broadcasted_iota(jnp.int32, (tokens, tokens), 1)
    earlier = (row < col).astype(F32)
    at = 0
    for per_expert in (16, 8):
        line = lax.broadcasted_iota(jnp.int32, (EXPERTS * per_expert, tokens), 0)
        expert = line // per_expert
        named = jnp.zeros(line.shape, F32)
        weight = jnp.zeros(line.shape, F32)
        for k in range(top):
            hit = ids[k:k + 1, :] == expert
            named += hit.astype(F32)
            weight += jnp.where(hit, weights[k:k + 1, :], 0.0)
        before = jnp.dot(named, earlier, preferred_element_type=F32)
        for base in range(0, 16, per_expert):
            slot = (line % per_expert + base).astype(F32)
            picks_ref[at:at + line.shape[0], :] = jnp.where(before == slot, weight, 0.0)
            at += line.shape[0]


def front_kernel(core_ref, ids_hbm, weights_hbm, residual_hbm, ctx_hbm, grad_hbm,
                 hid_hbm, gate_hbm, up_hbm, gw_hbm, uw_hbm,
                 own_ref, send_ref, rows_ref, picks_ref, residual_ref,
                 ids, weights, ctx, grad, hid, gate, up, gw, uw, gate_term, up_term, acc, sems):
    rows = ctx.shape[0]
    half = rows // 2
    full = rows + half
    slots, hidden = hid.shape
    cuts = range(0, hidden, HIDDEN_PART)
    copies = []

    def begin(source, target):
        copy = pltpu.make_async_copy(source, target, sems.at[len(copies)])
        copies.append(copy)
        copy.start()
        return copy

    def fetch(source, target, start, size):
        at = pl.ds(start, size)
        return begin(source.at[:, at], target.at[:, at])

    routes = [begin(ids_hbm, ids), begin(weights_hbm, weights)]
    width = grad.shape[1] // GRAD_PARTS
    ctx_copy = begin(ctx_hbm, ctx)
    grad_copies = [fetch(grad_hbm, grad, part * width, width) for part in range(GRAD_PARTS)]
    pairs = ((hid_hbm, hid), (gate_hbm, gate), (up_hbm, up), (gw_hbm, gw), (uw_hbm, uw))
    expert_copies = [
        [fetch(source, target, cut, min(HIDDEN_PART, hidden - cut)) for source, target in pairs]
        for cut in cuts
    ]
    residual_copy = begin(residual_hbm, residual_ref)

    for copy in routes:
        copy.wait()
    write_picks(ids[...], weights[...], picks_ref)
    ctx_copy.wait()
    core = core_ref[0]
    left = low_lanes(half)
    each = width // (2 * rows)
    for part in range(GRAD_PARTS):
        grad_copies[part].wait()
        for pair in range(part * each, (part + 1) * each):
            prod = jnp.dot(
                ctx[...], grad[:, pair * 2 * rows:(pair + 1) * 2 * rows],
                preferred_element_type=F32,
            )
            even, middle, odd = (prod[:, k * LANES:(k + 1) * LANES] for k in range(3))
            upper, lower = middle[:half], middle[half:]
            even_side = jnp.where(left, upper, pltpu.roll(lower, LANES // 2, 1))
            odd_side = jnp.where(left, pltpu.roll(upper, LANES // 2, 1), lower)
            main = slice(pair * full, pair * full + rows)
            rest = slice(pair * full + rows, (pair + 1) * full)
            own_ref[main, :] = jnp.where(core == 0, even, odd).astype(BF16)
            own_ref[rest, :] = jnp.where(core == 0, even_side, odd_side).astype(BF16)
            send_ref[main, :] = jnp.where(core == 0, odd, even).astype(BF16)
            send_ref[rest, :] = jnp.where(core == 0, odd_side, even_side).astype(BF16)

    dims = (((1,), (1,)), ((), ()))
    for copies_of_part, cut in zip(expert_copies, cuts):
        for copy in copies_of_part:
            copy.wait()
        cols = slice(cut, min(cut + HIDDEN_PART, hidden))
        for start in range(0, slots, 64):
            at = slice(start, start + 64)
            h = hid[at, cols].astype(F32)
            g = gate[at, cols].astype(F32)
            sig = 0.5 * jnp.tanh(0.5 * g) + 0.5
            silu = g * sig
            up_term[at, cols] = (h * silu).astype(BF16)
            gate_term[at, cols] = (
                h * up[at, cols].astype(F32) * (sig * (1.0 + g - silu))
            ).astype(BF16)
        prod = lax.dot_general(
            gate_term[:, cols], gw[:, cols], dims, preferred_element_type=F32
        ) + lax.dot_general(up_term[:, cols], uw[:, cols], dims, preferred_element_type=F32)
        acc[...] = prod if cut == 0 else acc[...] + prod
    rest = acc.shape[1] - LANES
    groups = slots // 16
    main = acc[:, :LANES].reshape(groups, 16, LANES)
    side = acc[:, LANES:].reshape(groups, 2, 8, rest)
    side = jnp.concatenate([side[:, 0], side[:, 1]], axis=-1)
    packed = jnp.concatenate([main, side], axis=1)
    rows_ref[...] = packed.reshape(groups * 24, LANES).astype(BF16)
    residual_copy.wait()


def front(core, ids, weights, residual, ctx, grad, *experts):
    rows, tokens = ctx.shape
    top, routed = ids.shape
    out_rows = grad.shape[1] * rows // LANES // 2
    slots, hidden = experts[0].shape
    arrays = (ctx, grad, *experts)
    pick_rows = 2 * 16 * EXPERTS
    return pl.pallas_call(
        front_kernel,
        in_specs=[pl.BlockSpec(memory_space=pltpu.SMEM)] + [in_hbm()] * 10,
        out_specs=[whole()] * 5,
        out_shape=[jax.ShapeDtypeStruct((out_rows, LANES), BF16)] * 2
        + [
            jax.ShapeDtypeStruct((slots * rows // LANES, LANES), BF16),
            jax.ShapeDtypeStruct((pick_rows, routed), F32),
            jax.ShapeDtypeStruct(residual.shape, BF16),
        ],
        scratch_shapes=[pltpu.VMEM((top, routed), jnp.int32), pltpu.VMEM((top, routed), F32)]
        + [pltpu.VMEM(array.shape, BF16) for array in arrays]
        + [pltpu.VMEM((slots, hidden), BF16)] * 2
        + [
            pltpu.VMEM((slots, rows), F32),
            pltpu.SemaphoreType.DMA((4 + GRAD_PARTS + 5 * pl.cdiv(hidden, HIDDEN_PART),)),
        ],
        compiler_params=params(40 * MIB),
        cost_estimate=pl.CostEstimate(
            flops=2 * tokens * rows * grad.shape[1] + 4 * slots * hidden * rows,
            bytes_accessed=14 * MIB,
            transcendentals=slots * hidden,
        ),
        name="front",
    )(core, *map(hold, (ids, weights, residual, *arrays)))


def chip_sum_kernel(place_ref, own_ref, got_ref, _, keep_ref, *send_refs, full):
    send_refs = send_refs[:3]
    place = place_ref[0]
    for y in range(keep_ref.shape[0] // full):
        at = slice(y * full, (y + 1) * full)
        for turn, ref in enumerate((keep_ref, *send_refs)):
            start = pl.multiple_of((4 * y + (place ^ turn)) * full, 32)
            block = pl.ds(start, full)
            total = own_ref[block, :].astype(F32) + got_ref[block, :].astype(F32)
            ref[at, :] = total.astype(ref.dtype)


def square_sum_kernel(y_ref, keep_ref, *refs, full):
    got, out = refs[:3], refs[3:]
    parts = keep_ref.shape[0] // full
    for step in range(parts):
        start = pl.multiple_of(((y_ref[0] + step) & (parts - 1)) * full, 32)
        block = pl.ds(start, full)
        total = keep_ref[block, :]
        for ref in got:
            total += ref[block, :].astype(F32)
        out[step][...] = total.astype(out[step].dtype)


def proj_final_kernel(core_ref, keep_ref, *refs):
    got, out_ref = refs[:-1], refs[-1]
    rows = out_ref.shape[0]
    core = core_ref[0]
    total = keep_ref[...]
    for ref in got:
        total += ref[...].astype(F32)
    main, packed = total[:rows], total[rows:]
    half = jnp.concatenate([packed, pltpu.roll(packed, LANES // 2, 1)], axis=0)
    turned = pltpu.roll(main, LANES // 2, 1)
    out_ref[:, :LANES] = jnp.where(core == 0, main, jnp.where(low_lanes(rows), half, turned))
    out_ref[:, LANES:] = jnp.where(core == 0, half, turned)[:, :rows - LANES]


def combine_kernel(picks_ref, residual_ref, got_ref, out_ref):
    experts = got_ref.shape[0] // 48
    got = got_ref[...].astype(F32).reshape(experts, 2, 24, LANES)
    both = got[:, 0] + got[:, 1]
    main = both[:, :16].reshape(experts * 16, LANES)
    side = both[:, 16:].reshape(experts * 8, LANES)

    def dot(start, values):
        return lax.dot_general(
            picks_ref[start:start + values.shape[0], :], values, (((0,), (0,)), ((), ())),
            precision=lax.Precision.HIGHEST, preferred_element_type=F32,
        )

    main_sum = dot(0, main)
    upper = dot(experts * 16, side)
    lower = dot(experts * 24, side)
    side_sum = upper + pltpu.roll(lower, LANES // 2, 1)
    rest = out_ref.shape[1] - LANES
    out_ref[:, :LANES] = (residual_ref[:, :LANES].astype(F32) + main_sum).astype(BF16)
    out_ref[:, LANES:] = (residual_ref[:, LANES:].astype(F32) + side_sum[:, :rest]).astype(BF16)


def shards(ids, weights, residual, hid, gate, up, gw, uw, ctx, grad, n_fsdp):
    me = lax.axis_index("fsdp")
    core = (me & 1).reshape(1)
    place = ((me >> 1) & 3).reshape(1)
    y2 = (me >> 3).reshape(1)
    rows = ctx.shape[1]
    full = rows * rows // LANES
    parts = n_fsdp // 8
    smem = pl.BlockSpec(memory_space=pltpu.SMEM)

    def swap(array, bits):
        return lax.ppermute(array, "fsdp", [(j, j ^ bits) for j in range(n_fsdp)])

    def shift(array, step):
        return lax.ppermute(
            array, "fsdp", [(j, (j + 8 * step) % n_fsdp) for j in range(n_fsdp)]
        )

    experts = (hid[0], gate[0], up[0], gw[0], uw[0])
    own, send, rows_out, picks, residual = front(
        core, ids.T, weights.T, residual, ctx.T, grad, *experts
    )
    got = swap(send, 1)

    quarter = jax.ShapeDtypeStruct((parts * full, LANES), BF16)
    keep, *square_send, rows_out = pl.pallas_call(
        functools.partial(chip_sum_kernel, full=full),
        in_specs=[smem, whole(), whole(), pl.BlockSpec(memory_space=pl.ANY)],
        out_specs=[whole()] * 4 + [pl.BlockSpec(memory_space=pl.ANY)],
        out_shape=[jax.ShapeDtypeStruct(quarter.shape, F32)] + [quarter] * 3
        + [jax.ShapeDtypeStruct(rows_out.shape, BF16)],
        input_output_aliases={3: 4},
        compiler_params=params(4 * MIB),
        name="chip_sum",
    )(place, own, got, rows_out)
    square_got = [swap(square_send[k - 1], 2 * k) for k in (1, 3, 2)]
    received = lax.all_to_all(
        rows_out.reshape(-1, 24, LANES), "ep", 0, 0, tiled=True
    ).reshape(rows_out.shape)
    block = jax.ShapeDtypeStruct((full, LANES), BF16)
    keep, *y_send = pl.pallas_call(
        functools.partial(square_sum_kernel, full=full),
        in_specs=[smem] + [whole()] * 4,
        out_specs=[whole()] * parts,
        out_shape=[jax.ShapeDtypeStruct(block.shape, F32)] + [block] * (parts - 1),
        compiler_params=params(4 * MIB),
        cost_estimate=pl.CostEstimate(flops=10**10, bytes_accessed=MIB, transcendentals=0),
        name="square_sum",
    )(y2, keep, *square_got)
    y_got = [shift(y_send[k - 1], k) for k in (2, 1, 3)]

    input_grad = pl.pallas_call(
        combine_kernel,
        in_specs=[whole()] * 3,
        out_specs=whole(),
        out_shape=jax.ShapeDtypeStruct(residual.shape, BF16),
        compiler_params=params(8 * MIB),
        name="combine",
    )(picks, residual, received)
    proj_weight_grad = pl.pallas_call(
        proj_final_kernel,
        in_specs=[smem] + [whole()] * parts,
        out_specs=whole(),
        out_shape=jax.ShapeDtypeStruct((rows, rows), F32),
        compiler_params=params(4 * MIB),
        name="proj_final",
    )(core, keep, *y_got)
    return input_grad, proj_weight_grad


def solution(mesh):
    return jax.shard_map(
        functools.partial(shards, n_fsdp=mesh.shape["fsdp"]),
        mesh=mesh,
        in_specs=(
            P("ep", None),
            P("ep", None),
            P("ep", "fsdp"),
            P("ep", None, None),
            P("ep", None, None),
            P("ep", None, None),
            P("ep", "fsdp", None),
            P("ep", "fsdp", None),
            P("fsdp", "ep"),
            P("fsdp", None),
        ),
        out_specs=(P("ep", "fsdp"), P("ep", "fsdp")),
        check_vma=False,
    )
```

time: 165 us -> 67.4 us (0.41)
  the two profiles are of different devices: /device:TPU:4 before, /device:TPU:40 now
where the time goes in v2:
time: 67.4 us; the launch traced here: 67 us
  starting transfers between devices  43.9 us (65%)
  waiting for transfers between devices  11.5 us (17%)
  Pallas kernels  10.8 us (16%)
  between operations  0.75 us (1%)
    all_to_all x1, starting transfers between devices, shards(): lax.all_to_all(rows_out.reshape(-1, 24, LANES), 'ep', 0, 0, tiled=True)  21.6 us
    ppermute x3, starting transfers between devices, shift(): lax.ppermute(array, 'fsdp', [(j, (j + 8 * step) % n_fsdp) for j in range(...  11.2 us
    ppermute x4, starting transfers between devices, swap(): return lax.ppermute(array, 'fsdp', [(j, j ^ bits) for j in range(n_fsdp)])  11.1 us
    pallas_call x1, Pallas kernels, front(): pl.pallas_call(front_kernel, in_specs=[pl.BlockSpec(memory_space=pltpu.SM...  7.91 us
    all_to_all x1, waiting for transfers between devices, shards(): lax.all_to_all(rows_out.reshape(-1, 24, LANES), 'ep', 0, 0, tiled=True)  5.02 us
    ppermute x3, waiting for transfers between devices, shift(): lax.ppermute(array, 'fsdp', [(j, (j + 8 * step) % n_fsdp) for j in range(...  3.45 us
    ppermute x4, waiting for transfers between devices, swap(): return lax.ppermute(array, 'fsdp', [(j, j ^ bits) for j in range(n_fsdp)])  3.03 us
  transfers between devices with their start and end apart: 8, of which 4 were waited for; matrix products, arithmetic and copies ran while one was open for 0% of the time, Pallas kernels for 1%

profile of v2, /device:TPU:40, one launch (start us, length us, event | category | flops | bytes accessed | tf_op | source)
XLA Modules:
  0.0 67.0 jit_solution(7673689670426582035)
XLA Ops:
  0.6 7.9 %front.1 = (bf16[4608,128]{1,0:T(8,128)(2,1)S(1)}, bf16[4608,128]{1,0:T(8,128)(2,1)}, bf16[768,128]{1,0:T(8,128)(2,1)}, f32[512,32]{1,0:T(8,128)S(1)}, bf16[32,192]{1,0:T(8,128)(2,1)S(1)}) custom-call(s32[1]{0:T(128)} %bitcast.core_ref, s32[4,32]{1,0:T(4,128)} %bitcast.20, f32[4,32]{1,0:T(4,128)} %bitcast.21, bf16[32,192]{1,0:T(8,128)(2,1)} %residual_hbm.1, ...), custom_call_target="tpu_custom_call" | custom-call | flops 1660944384 | bytes 14680064 | tf_op jit(solution)/shard_map/front/pallas_call | solution.py:153
  8.6 1.9 %collective-permute-start = (bf16[4608,128]{1,0:T(8,128)(2,1)}, bf16[4608,128]{1,0:T(8,128)(2,1)S(1)}, u32[]{:S(2)}, u32[]{:S(2)}) collective-permute-start(bf16[4608,128]{1,0:T(8,128)(2,1)} %get-tuple-element.19), channel_id=1, source_target_pairs={{0,32},{32,0},{64,96},{96,64},{128,160},{160,128},{192,224},{224,1... | collective-permute-start | bytes 3538952 | tf_op jit(solution)/shard_map/ppermute | solution.py:251
  10.5 3.0 %collective-permute-done.got_ref = bf16[4608,128]{1,0:T(8,128)(2,1)S(1)} collective-permute-done((bf16[4608,128]{1,0:T(8,128)(2,1)}, bf16[4608,128]{1,0:T(8,128)(2,1)S(1)}, u32[]{:S(2)}, u32[]{:S(2)}) %collective-permute-start) | collective-permute-done | bytes 1179680 | tf_op jit(solution)/shard_map/ppermute | solution.py:251
  13.5 0.9 %chip_sum.1 = (f32[1152,128]{1,0:T(8,128)S(1)}, bf16[1152,128]{1,0:T(8,128)(2,1)}, bf16[1152,128]{1,0:T(8,128)(2,1)S(1)}, bf16[1152,128]{1,0:T(8,128)(2,1)}, bf16[768,128]{1,0:T(8,128)(2,1)}) custom-call(s32[1]{0:T(128)} %bitcast.9.place_ref, bf16[4608,128]{1,0:T(8,128)(2,1)S(1)} %get-tuple-element.18.own_ref, ...), custom_call_target="tpu_custom_call", output_to_operand_aliasing={{4}: (3, {})} | custom-call | tf_op jit(solution)/shard_map/chip_sum/pallas_call | solution.py:265
  14.4 3.4 %collective-permute-start.1 = (bf16[1152,128]{1,0:T(8,128)(2,1)}, bf16[1152,128]{1,0:T(8,128)(2,1)S(1)}, u32[]{:S(2)}, u32[]{:S(2)}) collective-permute-start(bf16[1152,128]{1,0:T(8,128)(2,1)} %get-tuple-element.23), channel_id=1, source_target_pairs={{0,64},{32,96},{64,0},{96,32},{128,192},{160,224},{192,128},{224,1... | collective-permute-start | bytes 884744 | tf_op jit(solution)/shard_map/ppermute | solution.py:251
  17.8 3.2 %collective-permute-start.2 = (bf16[1152,128]{1,0:T(8,128)(2,1)}, bf16[1152,128]{1,0:T(8,128)(2,1)S(1)}, u32[]{:S(2)}, u32[]{:S(2)}) collective-permute-start(bf16[1152,128]{1,0:T(8,128)(2,1)} %get-tuple-element.24), channel_id=1, source_target_pairs={{0,192},{32,224},{64,128},{96,160},{128,64},{160,96},{192,0},{224,... | collective-permute-start | bytes 884744 | tf_op jit(solution)/shard_map/ppermute | solution.py:251
  21.1 2.6 %collective-permute-start.3 = (bf16[1152,128]{1,0:T(8,128)(2,1)S(1)}, bf16[1152,128]{1,0:T(8,128)(2,1)S(1)}, u32[]{:S(2)}, u32[]{:S(2)}) collective-permute-start(bf16[1152,128]{1,0:T(8,128)(2,1)S(1)} %get-tuple-element.25), channel_id=1, source_target_pairs={{0,128},{32,160},{64,192},{96,224},{128,0},{160,32},{192,64},{224,... | collective-permute-start | bytes 884744 | tf_op jit(solution)/shard_map/ppermute | solution.py:251
  23.7 21.6 %all-to-all-start = ((bf16[32,24,128]{2,1,0:T(8,128)(2,1)}), bf16[32,24,128]{2,1,0:T(8,128)(2,1)S(1)}, u32[]{:S(2)}, u32[]{:S(2)}) async-start(bf16[32,24,128]{2,1,0:T(8,128)(2,1)} %bitcast.10), calls=%async_computation | async-start | bytes 393216 | tf_op jit(solution)/shard_map/all_to_all | solution.py:276
  45.3 0.0 collective-permute-done.1.refs_0_
  45.3 0.0 collective-permute-done.2.refs_1_
  45.3 0.0 collective-permute-done.3.refs_2_
  45.3 0.1 square_sum.1
  45.5 3.2 %collective-permute-start.4 = (bf16[288,128]{1,0:T(8,128)(2,1)S(1)}, bf16[288,128]{1,0:T(8,128)(2,1)S(1)}, u32[]{:S(2)}, u32[]{:S(2)}) collective-permute-start(bf16[288,128]{1,0:T(8,128)(2,1)S(1)} %get-tuple-element.27), channel_id=1, source_target_pairs={{0,512},{32,544},{64,576},{96,608},{128,640},{160,672},{192,704},{... | collective-permute-start | bytes 221192 | tf_op jit(solution)/shard_map/ppermute | solution.py:254
  48.7 4.2 %collective-permute-start.5 = (bf16[288,128]{1,0:T(8,128)(2,1)S(1)}, bf16[288,128]{1,0:T(8,128)(2,1)S(1)}, u32[]{:S(2)}, u32[]{:S(2)}) collective-permute-start(bf16[288,128]{1,0:T(8,128)(2,1)S(1)} %get-tuple-element.28), channel_id=1, source_target_pairs={{0,256},{32,288},{64,320},{96,352},{128,384},{160,416},{192,448},{... | collective-permute-start | bytes 221192 | tf_op jit(solution)/shard_map/ppermute | solution.py:254
  52.9 3.8 %collective-permute-start.6 = (bf16[288,128]{1,0:T(8,128)(2,1)S(1)}, bf16[288,128]{1,0:T(8,128)(2,1)S(1)}, u32[]{:S(2)}, u32[]{:S(2)}) collective-permute-start(bf16[288,128]{1,0:T(8,128)(2,1)S(1)} %get-tuple-element.29), channel_id=1, source_target_pairs={{0,768},{32,800},{64,832},{96,864},{128,896},{160,928},{192,960},{... | collective-permute-start | bytes 221192 | tf_op jit(solution)/shard_map/ppermute | solution.py:254
  56.7 0.0 collective-permute-done.4.refs_0_
  56.7 2.9 %collective-permute-done.5.refs_1_ = bf16[288,128]{1,0:T(8,128)(2,1)S(1)} collective-permute-done((bf16[288,128]{1,0:T(8,128)(2,1)S(1)}, bf16[288,128]{1,0:T(8,128)(2,1)S(1)}, u32[]{:S(2)}, u32[]{:S(2)}) %collective-permute-start.5) | collective-permute-done | bytes 73760 | tf_op jit(solution)/shard_map/ppermute | solution.py:254
  59.6 0.6 collective-permute-done.6.refs_2_
  60.2 0.8 %proj_final.1 = f32[192,192]{1,0:T(8,128)} custom-call(s32[1]{0:T(128)} %bitcast.core_ref, f32[288,128]{1,0:T(8,128)S(1)} %get-tuple-element.26.keep_ref, bf16[288,128]{1,0:T(8,128)(2,1)S(1)} %collective-permute-done.4.refs_0_, bf16[288,128]{1,0:T(8,128)(2,1)S(1)} %collective-permute-done.5.refs_1_, bf16[288,128]{1,0:T(8,128)(2,1)S(1)} %collective-permute-done.6.refs_2_), custom_call_target="tpu_custom_call" | custom-call | tf_op jit(solution)/shard_map/proj_final/pallas_call | solution.py:299
  61.0 5.0 %all-to-all-done = bf16[32,24,128]{2,1,0:T(8,128)(2,1)S(1)} async-done(((bf16[32,24,128]{2,1,0:T(8,128)(2,1)}), bf16[32,24,128]{2,1,0:T(8,128)(2,1)S(1)}, u32[]{:S(2)}, u32[]{:S(2)}) %all-to-all-start) | async-done | bytes 196640 | tf_op jit(solution)/shard_map/all_to_all | solution.py:276
  66.0 1.0 %combine.1 = bf16[32,192]{1,0:T(8,128)(2,1)} custom-call(f32[512,32]{1,0:T(8,128)S(1)} %get-tuple-element.16.picks_ref, bf16[32,192]{1,0:T(8,128)(2,1)S(1)} %get-tuple-element.17.residual_ref, bf16[768,128]{1,0:T(8,128)(2,1)S(1)} %bitcast.13), custom_call_target="tpu_custom_call" | custom-call | tf_op jit(solution)/shard_map/combine/pallas_call | solution.py:291
Async XLA Ops:
  8.6 5.0 %collective-permute-start = (bf16[4608,128]{1,0:T(8,128)(2,1)}, bf16[4608,128]{1,0:T(8,128)(2,1)S(1)}, u32[]{:S(2)}, u32[]{:S(2)}) collective-permute-start(bf16[4608,128]{1,0:T(8,128)(2,1)} %get-tuple-element.19), channel_id=1, source_target_pairs={{0,32},{32,0},{64,96},{96,64},{128,160},{160,128},{192,224},{224,1... | collective-permute-start | bytes 3538952 | tf_op jit(solution)/shard_map/ppermute | solution.py:251
  14.4 30.9 %collective-permute-start.1 = (bf16[1152,128]{1,0:T(8,128)(2,1)}, bf16[1152,128]{1,0:T(8,128)(2,1)S(1)}, u32[]{:S(2)}, u32[]{:S(2)}) collective-permute-start(bf16[1152,128]{1,0:T(8,128)(2,1)} %get-tuple-element.23), channel_id=1, source_target_pairs={{0,64},{32,96},{64,0},{96,32},{128,192},{160,224},{192,128},{224,1... | collective-permute-start | bytes 884744 | tf_op jit(solution)/shard_map/ppermute | solution.py:251
  17.8 27.5 %collective-permute-start.2 = (bf16[1152,128]{1,0:T(8,128)(2,1)}, bf16[1152,128]{1,0:T(8,128)(2,1)S(1)}, u32[]{:S(2)}, u32[]{:S(2)}) collective-permute-start(bf16[1152,128]{1,0:T(8,128)(2,1)} %get-tuple-element.24), channel_id=1, source_target_pairs={{0,192},{32,224},{64,128},{96,160},{128,64},{160,96},{192,0},{224,... | collective-permute-start | bytes 884744 | tf_op jit(solution)/shard_map/ppermute | solution.py:251
  21.1 24.2 %collective-permute-start.3 = (bf16[1152,128]{1,0:T(8,128)(2,1)S(1)}, bf16[1152,128]{1,0:T(8,128)(2,1)S(1)}, u32[]{:S(2)}, u32[]{:S(2)}) collective-permute-start(bf16[1152,128]{1,0:T(8,128)(2,1)S(1)} %get-tuple-element.25), channel_id=1, source_target_pairs={{0,128},{32,160},{64,192},{96,224},{128,0},{160,32},{192,64},{224,... | collective-permute-start | bytes 884744 | tf_op jit(solution)/shard_map/ppermute | solution.py:251
  23.7 42.3 %all-to-all-start = ((bf16[32,24,128]{2,1,0:T(8,128)(2,1)}), bf16[32,24,128]{2,1,0:T(8,128)(2,1)S(1)}, u32[]{:S(2)}, u32[]{:S(2)}) async-start(bf16[32,24,128]{2,1,0:T(8,128)(2,1)} %bitcast.10), calls=%async_computation | async-start | bytes 393216 | tf_op jit(solution)/shard_map/all_to_all | solution.py:276
  45.5 11.2 %collective-permute-start.4 = (bf16[288,128]{1,0:T(8,128)(2,1)S(1)}, bf16[288,128]{1,0:T(8,128)(2,1)S(1)}, u32[]{:S(2)}, u32[]{:S(2)}) collective-permute-start(bf16[288,128]{1,0:T(8,128)(2,1)S(1)} %get-tuple-element.27), channel_id=1, source_target_pairs={{0,512},{32,544},{64,576},{96,608},{128,640},{160,672},{192,704},{... | collective-permute-start | bytes 221192 | tf_op jit(solution)/shard_map/ppermute | solution.py:254
  48.7 10.8 %collective-permute-start.5 = (bf16[288,128]{1,0:T(8,128)(2,1)S(1)}, bf16[288,128]{1,0:T(8,128)(2,1)S(1)}, u32[]{:S(2)}, u32[]{:S(2)}) collective-permute-start(bf16[288,128]{1,0:T(8,128)(2,1)S(1)} %get-tuple-element.28), channel_id=1, source_target_pairs={{0,256},{32,288},{64,320},{96,352},{128,384},{160,416},{192,448},{... | collective-permute-start | bytes 221192 | tf_op jit(solution)/shard_map/ppermute | solution.py:254
  52.9 7.2 %collective-permute-start.6 = (bf16[288,128]{1,0:T(8,128)(2,1)S(1)}, bf16[288,128]{1,0:T(8,128)(2,1)S(1)}, u32[]{:S(2)}, u32[]{:S(2)}) collective-permute-start(bf16[288,128]{1,0:T(8,128)(2,1)S(1)} %get-tuple-element.29), channel_id=1, source_target_pairs={{0,768},{32,800},{64,832},{96,864},{128,896},{160,928},{192,960},{... | collective-permute-start | bytes 221192 | tf_op jit(solution)/shard_map/ppermute | solution.py:254

commit v3 on v2

--- a/solution.py
+++ b/solution.py
@@ -12,7 +12,7 @@
 MIB = 1 << 20
 EXPERTS = 16
 GRAD_PARTS = 2
-HIDDEN_PART = 768
+HIDDEN_CUTS = (0, 384, 1152, 1920)
 
 
 def params(limit):
@@ -57,15 +57,13 @@
             at += line.shape[0]
 
 
-def front_kernel(core_ref, ids_hbm, weights_hbm, residual_hbm, ctx_hbm, grad_hbm,
-                 hid_hbm, gate_hbm, up_hbm, gw_hbm, uw_hbm,
-                 own_ref, send_ref, rows_ref, picks_ref, residual_ref,
-                 ids, weights, ctx, grad, hid, gate, up, gw, uw, gate_term, up_term, acc, sems):
+def front_kernel(core_ref, ids_hbm, weights_hbm, ctx_hbm, grad_hbm, *refs):
+    residual_hbm, own_ref, send_ref, picks_ref, residual_ref = refs[:5]
+    ids, weights, ctx, grad, packed, sems = refs[5:]
     rows = ctx.shape[0]
     half = rows // 2
     full = rows + half
-    slots, hidden = hid.shape
-    cuts = range(0, hidden, HIDDEN_PART)
+    width = grad.shape[1] // GRAD_PARTS
     copies = []
 
     def begin(source, target):
@@ -74,30 +72,20 @@
         copy.start()
         return copy
 
-    def fetch(source, target, start, size):
-        at = pl.ds(start, size)
-        return begin(source.at[:, at], target.at[:, at])
-
-    routes = [begin(ids_hbm, ids), begin(weights_hbm, weights)]
-    width = grad.shape[1] // GRAD_PARTS
-    ctx_copy = begin(ctx_hbm, ctx)
-    grad_copies = [fetch(grad_hbm, grad, part * width, width) for part in range(GRAD_PARTS)]
-    pairs = ((hid_hbm, hid), (gate_hbm, gate), (up_hbm, up), (gw_hbm, gw), (uw_hbm, uw))
-    expert_copies = [
-        [fetch(source, target, cut, min(HIDDEN_PART, hidden - cut)) for source, target in pairs]
-        for cut in cuts
-    ]
-    residual_copy = begin(residual_hbm, residual_ref)
-
-    for copy in routes:
+    small = [begin(ids_hbm, ids), begin(weights_hbm, weights), begin(ctx_hbm, ctx)]
+    parts = [pl.ds(part * width, width) for part in range(GRAD_PARTS)]
+    parts = [begin(grad_hbm.at[:, cols], grad.at[:, cols]) for cols in parts]
+    residual = begin(residual_hbm, residual_ref)
+
+    for copy in small:
         copy.wait()
     write_picks(ids[...], weights[...], picks_ref)
-    ctx_copy.wait()
     core = core_ref[0]
     left = low_lanes(half)
     each = width // (2 * rows)
+    leaving = []
     for part in range(GRAD_PARTS):
-        grad_copies[part].wait()
+        parts[part].wait()
         for pair in range(part * each, (part + 1) * each):
             prod = jnp.dot(
                 ctx[...], grad[:, pair * 2 * rows:(pair + 1) * 2 * rows],
@@ -111,70 +99,116 @@
             rest = slice(pair * full + rows, (pair + 1) * full)
             own_ref[main, :] = jnp.where(core == 0, even, odd).astype(BF16)
             own_ref[rest, :] = jnp.where(core == 0, even_side, odd_side).astype(BF16)
-            send_ref[main, :] = jnp.where(core == 0, odd, even).astype(BF16)
-            send_ref[rest, :] = jnp.where(core == 0, odd_side, even_side).astype(BF16)
-
-    dims = (((1,), (1,)), ((), ()))
-    for copies_of_part, cut in zip(expert_copies, cuts):
-        for copy in copies_of_part:
-            copy.wait()
-        cols = slice(cut, min(cut + HIDDEN_PART, hidden))
-        for start in range(0, slots, 64):
-            at = slice(start, start + 64)
-            h = hid[at, cols].astype(F32)
-            g = gate[at, cols].astype(F32)
-            sig = 0.5 * jnp.tanh(0.5 * g) + 0.5
-            silu = g * sig
-            up_term[at, cols] = (h * silu).astype(BF16)
-            gate_term[at, cols] = (
-                h * up[at, cols].astype(F32) * (sig * (1.0 + g - silu))
-            ).astype(BF16)
-        prod = lax.dot_general(
-            gate_term[:, cols], gw[:, cols], dims, preferred_element_type=F32
-        ) + lax.dot_general(up_term[:, cols], uw[:, cols], dims, preferred_element_type=F32)
-        acc[...] = prod if cut == 0 else acc[...] + prod
-    rest = acc.shape[1] - LANES
-    groups = slots // 16
-    main = acc[:, :LANES].reshape(groups, 16, LANES)
-    side = acc[:, LANES:].reshape(groups, 2, 8, rest)
-    side = jnp.concatenate([side[:, 0], side[:, 1]], axis=-1)
-    packed = jnp.concatenate([main, side], axis=1)
-    rows_ref[...] = packed.reshape(groups * 24, LANES).astype(BF16)
-    residual_copy.wait()
-
-
-def front(core, ids, weights, residual, ctx, grad, *experts):
+            packed[main, :] = jnp.where(core == 0, odd, even).astype(BF16)
+            packed[rest, :] = jnp.where(core == 0, odd_side, even_side).astype(BF16)
+        done = pl.ds(part * each * full, each * full)
+        leaving.append(begin(packed.at[done, :], send_ref.at[done, :]))
+    for copy in leaving:
+        copy.wait()
+    residual.wait()
+
+
+def front(core, ids, weights, ctx, grad, residual):
     rows, tokens = ctx.shape
     top, routed = ids.shape
     out_rows = grad.shape[1] * rows // LANES // 2
-    slots, hidden = experts[0].shape
-    arrays = (ctx, grad, *experts)
-    pick_rows = 2 * 16 * EXPERTS
     return pl.pallas_call(
         front_kernel,
-        in_specs=[pl.BlockSpec(memory_space=pltpu.SMEM)] + [in_hbm()] * 10,
-        out_specs=[whole()] * 5,
+        in_specs=[pl.BlockSpec(memory_space=pltpu.SMEM)] + [in_hbm()] * 5,
+        out_specs=[whole(), in_hbm(), whole(), whole()],
         out_shape=[jax.ShapeDtypeStruct((out_rows, LANES), BF16)] * 2
         + [
-            jax.ShapeDtypeStruct((slots * rows // LANES, LANES), BF16),
-            jax.ShapeDtypeStruct((pick_rows, routed), F32),
+            jax.ShapeDtypeStruct((2 * 16 * EXPERTS, routed), F32),
             jax.ShapeDtypeStruct(residual.shape, BF16),
         ],
-        scratch_shapes=[pltpu.VMEM((top, routed), jnp.int32), pltpu.VMEM((top, routed), F32)]
-        + [pltpu.VMEM(array.shape, BF16) for array in arrays]
+        scratch_shapes=[
+            pltpu.VMEM((top, routed), jnp.int32),
+            pltpu.VMEM((top, routed), F32),
+            pltpu.VMEM(ctx.shape, BF16),
+            pltpu.VMEM(grad.shape, BF16),
+            pltpu.VMEM((out_rows, LANES), BF16),
+            pltpu.SemaphoreType.DMA((4 + 2 * GRAD_PARTS,)),
+        ],
+        compiler_params=params(10 * MIB),
+        cost_estimate=pl.CostEstimate(
+            flops=2 * tokens * rows * grad.shape[1], bytes_accessed=6 * MIB, transcendentals=0
+        ),
+        name="front",
+    )(core, *map(hold, (ids, weights, ctx, grad, residual)))
+
+
+def expert_kernel(core_ref, *refs):
+    far, out_ref, near, (gate_term, up_term, acc, sems) = refs[:5], refs[5], refs[6:11], refs[11:]
+    hid_ref, gate_ref, up_ref, gw_ref, uw_ref = near
+    slots, hidden = hid_ref.shape
+    cuts = [*HIDDEN_CUTS, hidden]
+    parts = list(zip(cuts[:-1], cuts[1:]))
+    groups = []
+    for part, (low, high) in enumerate(parts):
+        cols = pl.ds(low, high - low)
+        groups.append([
+            pltpu.make_async_copy(source.at[:, cols], target.at[:, cols], sems.at[5 * part + k])
+            for k, (source, target) in enumerate(zip(far, near))
+        ])
+        for copy in groups[-1]:
+            copy.start()
+
+    for group, (low, high) in zip(groups, parts):
+        for copy in group:
+            copy.wait()
+
+        @pl.when(core_ref[0] >= 0)
+        def _(low=low, high=high):
+            cols = slice(low, high)
+            for start in range(0, slots, 64):
+                at = slice(start, start + 64)
+                hid = hid_ref[at, cols].astype(F32)
+                gate = gate_ref[at, cols].astype(F32)
+                sig = 0.5 * jnp.tanh(0.5 * gate) + 0.5
+                silu = gate * sig
+                up_term[at, cols] = (hid * silu).astype(BF16)
+                gate_term[at, cols] = (
+                    hid * up_ref[at, cols].astype(F32) * (sig * (1.0 + gate - silu))
+                ).astype(BF16)
+            dims = (((1,), (1,)), ((), ()))
+            prod = lax.dot_general(
+                gate_term[:, cols], gw_ref[:, cols], dims, preferred_element_type=F32
+            ) + lax.dot_general(
+                up_term[:, cols], uw_ref[:, cols], dims, preferred_element_type=F32
+            )
+            acc[...] = prod if low == 0 else acc[...] + prod
+
+    width = acc.shape[1]
+    count = slots // 16
+    main = acc[:, :LANES].reshape(count, 16, LANES)
+    side = acc[:, LANES:].reshape(count, 2, 8, width - LANES)
+    side = jnp.concatenate([side[:, 0], side[:, 1]], axis=-1)
+    packed = jnp.concatenate([main, side], axis=1)
+    out_ref[...] = packed.reshape(count * 24, LANES).astype(BF16)
+
+
+def expert_rows(core, *far):
+    slots, hidden = far[0].shape
+    width = far[3].shape[0]
+    return pl.pallas_call(
+        expert_kernel,
+        in_specs=[pl.BlockSpec(memory_space=pltpu.SMEM)] + [in_hbm()] * 5,
+        out_specs=whole(),
+        out_shape=jax.ShapeDtypeStruct((slots * width // LANES, LANES), BF16),
+        scratch_shapes=[pltpu.VMEM(array.shape, BF16) for array in far]
         + [pltpu.VMEM((slots, hidden), BF16)] * 2
         + [
-            pltpu.VMEM((slots, rows), F32),
-            pltpu.SemaphoreType.DMA((4 + GRAD_PARTS + 5 * pl.cdiv(hidden, HIDDEN_PART),)),
+            pltpu.VMEM((slots, width), F32),
+            pltpu.SemaphoreType.DMA((5 * len(HIDDEN_CUTS),)),
         ],
-        compiler_params=params(40 * MIB),
+        compiler_params=params(32 * MIB),
         cost_estimate=pl.CostEstimate(
-            flops=2 * tokens * rows * grad.shape[1] + 4 * slots * hidden * rows,
-            bytes_accessed=14 * MIB,
+            flops=4 * slots * hidden * width,
+            bytes_accessed=2 * hidden * (3 * slots + 2 * width),
             transcendentals=slots * hidden,
         ),
-        name="front",
-    )(core, *map(hold, (ids, weights, residual, *arrays)))
+        name="expert_rows",
+    )(core, *map(hold, far))
 
 
 def chip_sum_kernel(place_ref, own_ref, got_ref, _, keep_ref, *send_refs, full):
@@ -201,8 +235,7 @@
         out[step][...] = total.astype(out[step].dtype)
 
 
-def proj_final_kernel(core_ref, keep_ref, *refs):
-    got, out_ref = refs[:-1], refs[-1]
+def write_proj(core_ref, keep_ref, got, out_ref):
     rows = out_ref.shape[0]
     core = core_ref[0]
     total = keep_ref[...]
@@ -215,7 +248,7 @@
     out_ref[:, LANES:] = jnp.where(core == 0, half, turned)[:, :rows - LANES]
 
 
-def combine_kernel(picks_ref, residual_ref, got_ref, out_ref):
+def write_input(picks_ref, residual_ref, got_ref, out_ref):
     experts = got_ref.shape[0] // 48
     got = got_ref[...].astype(F32).reshape(experts, 2, 24, LANES)
     both = got[:, 0] + got[:, 1]
@@ -235,6 +268,12 @@
     rest = out_ref.shape[1] - LANES
     out_ref[:, :LANES] = (residual_ref[:, :LANES].astype(F32) + main_sum).astype(BF16)
     out_ref[:, LANES:] = (residual_ref[:, LANES:].astype(F32) + side_sum[:, :rest]).astype(BF16)
+
+
+def last_kernel(core_ref, keep_ref, *refs):
+    got, routed, (input_ref, proj_ref) = refs[:-5], refs[-5:-2], refs[-2:]
+    write_input(*routed, input_ref)
+    write_proj(core_ref, keep_ref, got, proj_ref)
 
 
 def shards(ids, weights, residual, hid, gate, up, gw, uw, ctx, grad, n_fsdp):
@@ -256,10 +295,9 @@
         )
 
     experts = (hid[0], gate[0], up[0], gw[0], uw[0])
-    own, send, rows_out, picks, residual = front(
-        core, ids.T, weights.T, residual, ctx.T, grad, *experts
-    )
+    own, send, picks, residual = front(core, ids.T, weights.T, ctx.T, grad, residual)
     got = swap(send, 1)
+    rows_out = expert_rows(core, *experts)
 
     quarter = jax.ShapeDtypeStruct((parts * full, LANES), BF16)
     keep, *square_send, rows_out = pl.pallas_call(
@@ -286,24 +324,19 @@
         cost_estimate=pl.CostEstimate(flops=10**10, bytes_accessed=MIB, transcendentals=0),
         name="square_sum",
     )(y2, keep, *square_got)
-    y_got = [shift(y_send[k - 1], k) for k in (2, 1, 3)]
-
-    input_grad = pl.pallas_call(
-        combine_kernel,
-        in_specs=[whole()] * 3,
-        out_specs=whole(),
-        out_shape=jax.ShapeDtypeStruct(residual.shape, BF16),
+    y_got = [shift(y_send[k - 1], k) for k in (1, 3, 2)]
+
+    input_grad, proj_weight_grad = pl.pallas_call(
+        last_kernel,
+        in_specs=[smem] + [whole()] * (parts + 3),
+        out_specs=[whole()] * 2,
+        out_shape=[
+            jax.ShapeDtypeStruct(residual.shape, BF16),
+            jax.ShapeDtypeStruct((rows, rows), F32),
+        ],
         compiler_params=params(8 * MIB),
-        name="combine",
-    )(picks, residual, received)
-    proj_weight_grad = pl.pallas_call(
-        proj_final_kernel,
-        in_specs=[smem] + [whole()] * parts,
-        out_specs=whole(),
-        out_shape=jax.ShapeDtypeStruct((rows, rows), F32),
-        compiler_params=params(4 * MIB),
-        name="proj_final",
-    )(core, keep, *y_got)
+        name="last",
+    )(core, keep, *y_got, picks, residual, received)
     return input_grad, proj_weight_grad
 
 

time: 67.4 us -> 66.5 us (0.987)
  waiting for transfers between devices: 11.5 us -> 9.26 us
  Pallas kernels: 10.8 us -> 11.8 us
    pallas_call x2, Pallas kernels: 1.8 us -> 7.08 us  [the longest x1 5.99 us: expert_rows(): pl.pallas_call(expert_kernel, in_specs=[pl.BlockSpec(memory_space=pltpu.S...]
    pallas_call x1, Pallas kernels: 7.91 us -> 3.66 us  [front(): pl.pallas_call(front_kernel, in_specs=[pl.BlockSpec(memory_space=pltpu.SM...]
    ppermute x3, waiting for transfers between devices: 3.45 us -> 6.86 us  [shift(): lax.ppermute(array, 'fsdp', [(j, (j + 8 * step) % n_fsdp) for j in range(...]
    ppermute x4, waiting for transfers between devices: 3.03 us -> 0.01 us  [swap(): return lax.ppermute(array, 'fsdp', [(j, j ^ bits) for j in range(n_fsdp)])]
    all_to_all x1, waiting for transfers between devices: 5.02 us -> 2.39 us  [shards(): lax.all_to_all(rows_out.reshape(-1, 24, LANES), 'ep', 0, 0, tiled=True)]
  transfers between devices with their start and end apart: 8 -> 8, of which waited for: 4 -> 2; matrix products, arithmetic and copies ran while one was open for 0% -> 0% of each run, Pallas kernels for 1% -> 9%
where the time goes in v3:
time: 66.5 us; the launch traced here: 66.2 us
  starting transfers between devices  44.3 us (67%)
  Pallas kernels  11.8 us (18%)
  waiting for transfers between devices  9.26 us (14%)
  between operations  0.77 us (1%)
    all_to_all x1, starting transfers between devices, shards(): lax.all_to_all(rows_out.reshape(-1, 24, LANES), 'ep', 0, 0, tiled=True)  21.6 us
    ppermute x3, starting transfers between devices, shift(): lax.ppermute(array, 'fsdp', [(j, (j + 8 * step) % n_fsdp) for j in range(...  11.6 us
    ppermute x4, starting transfers between devices, swap(): return lax.ppermute(array, 'fsdp', [(j, j ^ bits) for j in range(n_fsdp)])  11.1 us
    ppermute x3, waiting for transfers between devices, shift(): lax.ppermute(array, 'fsdp', [(j, (j + 8 * step) % n_fsdp) for j in range(...  6.86 us
    pallas_call x1, Pallas kernels, expert_rows(): pl.pallas_call(expert_kernel, in_specs=[pl.BlockSpec(memory_space=pltpu.S...  5.99 us
    pallas_call x1, Pallas kernels, front(): pl.pallas_call(front_kernel, in_specs=[pl.BlockSpec(memory_space=pltpu.SM...  3.66 us
    all_to_all x1, waiting for transfers between devices, shards(): lax.all_to_all(rows_out.reshape(-1, 24, LANES), 'ep', 0, 0, tiled=True)  2.39 us
  transfers between devices with their start and end apart: 8, of which 2 were waited for; matrix products, arithmetic and copies ran while one was open for 0% of the time, Pallas kernels for 9%

profile of v3, /device:TPU:40, one launch (start us, length us, event | category | flops | bytes accessed | tf_op | source)
XLA Modules:
  0.0 66.2 jit_solution(15756912599858289646)
XLA Ops:
  0.6 3.7 %front.1 = (bf16[4608,128]{1,0:T(8,128)(2,1)S(1)}, bf16[4608,128]{1,0:T(8,128)(2,1)}, f32[512,32]{1,0:T(8,128)S(1)}, bf16[32,192]{1,0:T(8,128)(2,1)S(1)}) custom-call(s32[1]{0:T(128)} %bitcast.core_ref, s32[4,32]{1,0:T(4,128)} %bitcast.20, f32[4,32]{1,0:T(4,128)} %bitcast.21, bf16[192,256]{1,0:T(8,128)(2,1)} %bitcast.19, bf16[256,6144]{1,0:T(8,128)(2,1)} %grad_hbm.1, ...), custom_call_target="tpu_custom_call" | custom-call | flops 603979776 | bytes 6291456 | tf_op jit(solution)/shard_map/front/pallas_call | solution.py:115
  4.3 1.9 %collective-permute-start = (bf16[4608,128]{1,0:T(8,128)(2,1)}, bf16[4608,128]{1,0:T(8,128)(2,1)S(1)}, u32[]{:S(2)}, u32[]{:S(2)}) collective-permute-start(bf16[4608,128]{1,0:T(8,128)(2,1)} %get-tuple-element.16), channel_id=1, source_target_pairs={{0,32},{32,0},{64,96},{96,64},{128,160},{160,128},{192,224},{224,1... | collective-permute-start | bytes 3538952 | tf_op jit(solution)/shard_map/ppermute | solution.py:290
  6.2 6.0 %expert_rows.1._ = bf16[768,128]{1,0:T(8,128)(2,1)} custom-call(s32[1]{0:T(128)} %bitcast.core_ref, bf16[512,2688]{1,0:T(8,128)(2,1)} %bitcast.14, bf16[512,2688]{1,0:T(8,128)(2,1)} %bitcast.15, bf16[512,2688]{1,0:T(8,128)(2,1)} %bitcast.16, bf16[192,2688]{1,0:T(8,128)(2,1)} %bitcast.17, bf16[192,2688]{1,0:T(8,128)(2,1)} %bitcast.18), custom_call_target="tpu_custom_call" | custom-call | flops 1056964608 | bytes 10321920 | tf_op jit(solution)/shard_map/expert_rows/pallas_call | solution.py:193
  12.2 0.0 collective-permute-done.got_ref
  12.2 0.9 %chip_sum.1 = (f32[1152,128]{1,0:T(8,128)S(1)}, bf16[1152,128]{1,0:T(8,128)(2,1)}, bf16[1152,128]{1,0:T(8,128)(2,1)S(1)}, bf16[1152,128]{1,0:T(8,128)(2,1)}, bf16[768,128]{1,0:T(8,128)(2,1)}) custom-call(s32[1]{0:T(128)} %bitcast.2.place_ref, bf16[4608,128]{1,0:T(8,128)(2,1)S(1)} %get-tuple-element.15.own_ref, ...), custom_call_target="tpu_custom_call", output_to_operand_aliasing={{4}: (3, {})} | custom-call | tf_op jit(solution)/shard_map/chip_sum/pallas_call | solution.py:303
  13.2 3.4 %collective-permute-start.1 = (bf16[1152,128]{1,0:T(8,128)(2,1)}, bf16[1152,128]{1,0:T(8,128)(2,1)S(1)}, u32[]{:S(2)}, u32[]{:S(2)}) collective-permute-start(bf16[1152,128]{1,0:T(8,128)(2,1)} %get-tuple-element.18), channel_id=1, source_target_pairs={{0,64},{32,96},{64,0},{96,32},{128,192},{160,224},{192,128},{224,1... | collective-permute-start | bytes 884744 | tf_op jit(solution)/shard_map/ppermute | solution.py:290
  16.6 3.2 %collective-permute-start.2 = (bf16[1152,128]{1,0:T(8,128)(2,1)}, bf16[1152,128]{1,0:T(8,128)(2,1)S(1)}, u32[]{:S(2)}, u32[]{:S(2)}) collective-permute-start(bf16[1152,128]{1,0:T(8,128)(2,1)} %get-tuple-element.19), channel_id=1, source_target_pairs={{0,192},{32,224},{64,128},{96,160},{128,64},{160,96},{192,0},{224,... | collective-permute-start | bytes 884744 | tf_op jit(solution)/shard_map/ppermute | solution.py:290
  19.8 2.6 %collective-permute-start.3 = (bf16[1152,128]{1,0:T(8,128)(2,1)S(1)}, bf16[1152,128]{1,0:T(8,128)(2,1)S(1)}, u32[]{:S(2)}, u32[]{:S(2)}) collective-permute-start(bf16[1152,128]{1,0:T(8,128)(2,1)S(1)} %get-tuple-element.20), channel_id=1, source_target_pairs={{0,128},{32,160},{64,192},{96,224},{128,0},{160,32},{192,64},{224,... | collective-permute-start | bytes 884744 | tf_op jit(solution)/shard_map/ppermute | solution.py:290
  22.4 21.6 %all-to-all-start = ((bf16[32,24,128]{2,1,0:T(8,128)(2,1)}), bf16[32,24,128]{2,1,0:T(8,128)(2,1)S(1)}, u32[]{:S(2)}, u32[]{:S(2)}) async-start(bf16[32,24,128]{2,1,0:T(8,128)(2,1)} %bitcast.11), calls=%async_computation | async-start | bytes 393216 | tf_op jit(solution)/shard_map/all_to_all | solution.py:314
  44.0 0.0 collective-permute-done.1.refs_0_
  44.1 0.0 collective-permute-done.2.refs_1_
  44.1 0.0 collective-permute-done.3.refs_2_
  44.1 0.1 square_sum.1
  44.2 2.7 %collective-permute-start.4 = (bf16[288,128]{1,0:T(8,128)(2,1)S(1)}, bf16[288,128]{1,0:T(8,128)(2,1)S(1)}, u32[]{:S(2)}, u32[]{:S(2)}) collective-permute-start(bf16[288,128]{1,0:T(8,128)(2,1)S(1)} %get-tuple-element.22), channel_id=1, source_target_pairs={{0,256},{32,288},{64,320},{96,352},{128,384},{160,416},{192,448},{... | collective-permute-start | bytes 221192 | tf_op jit(solution)/shard_map/ppermute | solution.py:293
  46.9 5.3 %collective-permute-start.5 = (bf16[288,128]{1,0:T(8,128)(2,1)S(1)}, bf16[288,128]{1,0:T(8,128)(2,1)S(1)}, u32[]{:S(2)}, u32[]{:S(2)}) collective-permute-start(bf16[288,128]{1,0:T(8,128)(2,1)S(1)} %get-tuple-element.23), channel_id=1, source_target_pairs={{0,768},{32,800},{64,832},{96,864},{128,896},{160,928},{192,960},{... | collective-permute-start | bytes 221192 | tf_op jit(solution)/shard_map/ppermute | solution.py:293
  52.2 3.6 %collective-permute-start.6 = (bf16[288,128]{1,0:T(8,128)(2,1)S(1)}, bf16[288,128]{1,0:T(8,128)(2,1)S(1)}, u32[]{:S(2)}, u32[]{:S(2)}) collective-permute-start(bf16[288,128]{1,0:T(8,128)(2,1)S(1)} %get-tuple-element.24), channel_id=1, source_target_pairs={{0,512},{32,544},{64,576},{96,608},{128,640},{160,672},{192,704},{... | collective-permute-start | bytes 221192 | tf_op jit(solution)/shard_map/ppermute | solution.py:293
  55.8 0.0 collective-permute-done.4.refs_0_
  55.8 0.0 collective-permute-done.5.refs_1_
  55.8 6.9 %collective-permute-done.6.refs_2_ = bf16[288,128]{1,0:T(8,128)(2,1)S(1)} collective-permute-done((bf16[288,128]{1,0:T(8,128)(2,1)S(1)}, bf16[288,128]{1,0:T(8,128)(2,1)S(1)}, u32[]{:S(2)}, u32[]{:S(2)}) %collective-permute-start.6) | collective-permute-done | bytes 73760 | tf_op jit(solution)/shard_map/ppermute | solution.py:293
  62.7 2.4 %all-to-all-done = bf16[32,24,128]{2,1,0:T(8,128)(2,1)S(1)} async-done(((bf16[32,24,128]{2,1,0:T(8,128)(2,1)}), bf16[32,24,128]{2,1,0:T(8,128)(2,1)S(1)}, u32[]{:S(2)}, u32[]{:S(2)}) %all-to-all-start) | async-done | bytes 196640 | tf_op jit(solution)/shard_map/all_to_all | solution.py:314
  65.1 1.1 %last.1 = (bf16[32,192]{1,0:T(8,128)(2,1)}, f32[192,192]{1,0:T(8,128)}) custom-call(s32[1]{0:T(128)} %bitcast.core_ref, f32[288,128]{1,0:T(8,128)S(1)} %get-tuple-element.21.keep_ref, bf16[288,128]{1,0:T(8,128)(2,1)S(1)} %collective-permute-done.4.refs_0_, bf16[288,128]{1,0:T(8,128)(2,1)S(1)} %collective-permute-done.5.refs_1_, ...), custom_call_target="tpu_custom_call" | custom-call | tf_op jit(solution)/shard_map/last/pallas_call | solution.py:329
Async XLA Ops:
  4.3 7.9 %collective-permute-start = (bf16[4608,128]{1,0:T(8,128)(2,1)}, bf16[4608,128]{1,0:T(8,128)(2,1)S(1)}, u32[]{:S(2)}, u32[]{:S(2)}) collective-permute-start(bf16[4608,128]{1,0:T(8,128)(2,1)} %get-tuple-element.16), channel_id=1, source_target_pairs={{0,32},{32,0},{64,96},{96,64},{128,160},{160,128},{192,224},{224,1... | collective-permute-start | bytes 3538952 | tf_op jit(solution)/shard_map/ppermute | solution.py:290
  13.2 30.9 %collective-permute-start.1 = (bf16[1152,128]{1,0:T(8,128)(2,1)}, bf16[1152,128]{1,0:T(8,128)(2,1)S(1)}, u32[]{:S(2)}, u32[]{:S(2)}) collective-permute-start(bf16[1152,128]{1,0:T(8,128)(2,1)} %get-tuple-element.18), channel_id=1, source_target_pairs={{0,64},{32,96},{64,0},{96,32},{128,192},{160,224},{192,128},{224,1... | collective-permute-start | bytes 884744 | tf_op jit(solution)/shard_map/ppermute | solution.py:290
  16.6 27.5 %collective-permute-start.2 = (bf16[1152,128]{1,0:T(8,128)(2,1)}, bf16[1152,128]{1,0:T(8,128)(2,1)S(1)}, u32[]{:S(2)}, u32[]{:S(2)}) collective-permute-start(bf16[1152,128]{1,0:T(8,128)(2,1)} %get-tuple-element.19), channel_id=1, source_target_pairs={{0,192},{32,224},{64,128},{96,160},{128,64},{160,96},{192,0},{224,... | collective-permute-start | bytes 884744 | tf_op jit(solution)/shard_map/ppermute | solution.py:290
  19.8 24.2 %collective-permute-start.3 = (bf16[1152,128]{1,0:T(8,128)(2,1)S(1)}, bf16[1152,128]{1,0:T(8,128)(2,1)S(1)}, u32[]{:S(2)}, u32[]{:S(2)}) collective-permute-start(bf16[1152,128]{1,0:T(8,128)(2,1)S(1)} %get-tuple-element.20), channel_id=1, source_target_pairs={{0,128},{32,160},{64,192},{96,224},{128,0},{160,32},{192,64},{224,... | collective-permute-start | bytes 884744 | tf_op jit(solution)/shard_map/ppermute | solution.py:290
  22.4 42.7 %all-to-all-start = ((bf16[32,24,128]{2,1,0:T(8,128)(2,1)}), bf16[32,24,128]{2,1,0:T(8,128)(2,1)S(1)}, u32[]{:S(2)}, u32[]{:S(2)}) async-start(bf16[32,24,128]{2,1,0:T(8,128)(2,1)} %bitcast.11), calls=%async_computation | async-start | bytes 393216 | tf_op jit(solution)/shard_map/all_to_all | solution.py:314
  44.2 11.6 %collective-permute-start.4 = (bf16[288,128]{1,0:T(8,128)(2,1)S(1)}, bf16[288,128]{1,0:T(8,128)(2,1)S(1)}, u32[]{:S(2)}, u32[]{:S(2)}) collective-permute-start(bf16[288,128]{1,0:T(8,128)(2,1)S(1)} %get-tuple-element.22), channel_id=1, source_target_pairs={{0,256},{32,288},{64,320},{96,352},{128,384},{160,416},{192,448},{... | collective-permute-start | bytes 221192 | tf_op jit(solution)/shard_map/ppermute | solution.py:293
  46.9 8.9 %collective-permute-start.5 = (bf16[288,128]{1,0:T(8,128)(2,1)S(1)}, bf16[288,128]{1,0:T(8,128)(2,1)S(1)}, u32[]{:S(2)}, u32[]{:S(2)}) collective-permute-start(bf16[288,128]{1,0:T(8,128)(2,1)S(1)} %get-tuple-element.23), channel_id=1, source_target_pairs={{0,768},{32,800},{64,832},{96,864},{128,896},{160,928},{192,960},{... | collective-permute-start | bytes 221192 | tf_op jit(solution)/shard_map/ppermute | solution.py:293
  52.2 10.5 %collective-permute-start.6 = (bf16[288,128]{1,0:T(8,128)(2,1)S(1)}, bf16[288,128]{1,0:T(8,128)(2,1)S(1)}, u32[]{:S(2)}, u32[]{:S(2)}) collective-permute-start(bf16[288,128]{1,0:T(8,128)(2,1)S(1)} %get-tuple-element.24), channel_id=1, source_target_pairs={{0,512},{32,544},{64,576},{96,608},{128,640},{160,672},{192,704},{... | collective-permute-start | bytes 221192 | tf_op jit(solution)/shard_map/ppermute | solution.py:293
